TPU v7x, 32 devices: a whole 2x2x4 slice. The times are simulated.
32 devices in a mesh: sub: 2 (over x), row: 4 (over y, core), col: 4 (over z).
Axes of the slice: x: 2, y: 2, z: 4, core: 2. Of those that a mesh axis runs over, the one named last changes fastest.
Arguments:
- front_panel: bfloat16 [16384, 3072], P(('sub', 'row', 'col')), may hold values from -6 to 6
- tile_inverse: bfloat16 [12, 256, 256], replicated
- front_trailing: float32 [16384, 16384], P(('sub', 'row'), 'col'), may hold values from -6 to 6
- child_update: bfloat16 [2, 5120, 5120], P('sub', 'col', 'row'), may hold values from -6 to 6
- child_map: int32 [2, 20], replicated, may hold values from 0 to 63, as said below
- pattern: int32 [64, 64], replicated, may hold values from 0 to 1, as said below
Outputs:
- factor: bfloat16 [16384, 3072], P(('sub', 'row', 'col'))
- trailing: float32 [16384, 16384], P(('sub', 'row'), 'col')
Inputs may be any that keep to these rules, and one draw needn't show every extreme that they name: `child_map`: each row lists 20 distinct parent tiles in increasing order; the first child's row always holds tile 0 and tile 64 - 1. `pattern`: symmetric, with ones on the diagonal.
All inputs are finite; a program needn't handle non-finite values.
Results may differ from a plain program's by a relative error of at most 0.001.
Values may be sent and summed in bfloat16 or wider, within the bound.
No kernel may reach another device: no remote copies, remote signals or barrier semaphores. Data moves between devices by JAX's collectives and lax.ppermute only.
A program may use at most 320 MiB of HBM per device.

v0:
```python
import jax
import jax.numpy as jnp
from jax import lax
from jax.sharding import PartitionSpec as P


def spread(value, axis, source):
    kept = jnp.where(lax.axis_index(axis) == source, value, 0).astype(value.dtype)
    return lax.psum(kept, axis)


def partner(value, axis, distance):
    mask = 2**distance
    pairs = [(source, source ^ mask) for source in range(lax.axis_size(axis))]
    return lax.ppermute(value, axis, pairs)


def apply_inverse(panel_rows, inverses):
    row_count = panel_rows.shape[0]
    tile_count = inverses.shape[0]
    tile_size = inverses.shape[1]
    shaped = panel_rows.reshape(row_count, tile_count, tile_size)
    scaled = jnp.einsum("rkt,kts->rks", shaped, inverses, preferred_element_type=jnp.float32)
    return scaled.astype(jnp.bfloat16).reshape(row_count, tile_count * tile_size)


def place_columns(child_block, tile_map, parent_tiles, tile_size):
    row_count = child_block.shape[0]
    tile_count = tile_map.shape[0]
    wanted = jnp.arange(parent_tiles, dtype=jnp.int32)
    onehot = (tile_map[:, None] == wanted[None, :]).astype(jnp.bfloat16)
    placed = jnp.einsum(
        "rjt,jq->rqt",
        child_block.reshape(row_count, tile_count, tile_size),
        onehot,
        preferred_element_type=jnp.float32,
    )
    return placed.astype(jnp.bfloat16).reshape(row_count, parent_tiles * tile_size)


def pick_rows(child_block, tile_map, grid_block, tile_rows, tile_size):
    tile_count = tile_map.shape[0]
    width_cols = child_block.shape[1]
    wanted = grid_block * tile_rows + jnp.arange(tile_rows, dtype=jnp.int32)
    onehot = (tile_map[:, None] == wanted[None, :]).astype(jnp.bfloat16)
    picked = jnp.einsum(
        "itx,ip->ptx",
        child_block.reshape(tile_count, tile_size, width_cols),
        onehot,
        preferred_element_type=jnp.float32,
    )
    return picked.reshape(tile_rows * tile_size, width_cols)


def per_device(front_panel, tile_inverse, front_trailing, child_update, child_map, pattern):
    tile_size = tile_inverse.shape[1]
    parent_tiles = pattern.shape[0]
    block_rows = front_trailing.shape[0]
    block_cols = front_trailing.shape[1]
    tile_rows = block_rows // tile_size
    tile_cols = block_cols // tile_size
    sub_index = lax.axis_index("sub")
    row_index = lax.axis_index("row")
    col_index = lax.axis_index("col")
    rows_count = lax.axis_size("row")
    grid_row = sub_index * rows_count + row_index
    factor = apply_inverse(front_panel, tile_inverse)
    front_rows = lax.all_gather(front_panel, "col", axis=0, tiled=True)
    row_panel = apply_inverse(front_rows, tile_inverse)
    share_rows = min(block_rows, block_cols)
    pieces = []
    for part_index in range(block_cols // share_rows):
        first_row = col_index * block_cols + part_index * share_rows
        source = first_row // block_rows
        offset = first_row % block_rows
        share_block = lax.dynamic_slice_in_dim(row_panel, offset, share_rows, 0)
        pieces.append(spread(share_block, ("sub", "row"), source))
    column_panel = pieces[0] if len(pieces) == 1 else jnp.concatenate(pieces, axis=0)
    own_map = lax.dynamic_index_in_dim(child_map, sub_index, 0, keepdims=False)
    own_child = child_update[0]
    gathered = lax.all_gather(own_child, "row", axis=1, tiled=True)
    placed = place_columns(gathered, own_map, parent_tiles, tile_size)
    child_rows = lax.all_to_all(placed, "col", split_axis=1, concat_axis=0, tiled=True)
    own_part = pick_rows(child_rows, own_map, grid_row, tile_rows, tile_size)
    other_block = (1 - sub_index) * rows_count + row_index
    sibling_part = pick_rows(child_rows, own_map, other_block, tile_rows, tile_size).astype(
        jnp.bfloat16
    )
    received = partner(sibling_part, "sub", 0)
    extend = own_part + received.astype(jnp.float32)
    local_mask = lax.dynamic_slice(
        pattern, (grid_row * tile_rows, col_index * tile_cols), (tile_rows, tile_cols)
    )
    product = lax.dot_general(
        row_panel, column_panel, (((1,), (1,)), ((), ())), preferred_element_type=jnp.float32
    )
    weights = local_mask.astype(jnp.float32)
    masked = (
        product.reshape(tile_rows, tile_size, tile_cols, tile_size) * weights[:, None, :, None]
    ).reshape(block_rows, block_cols)
    trailing = front_trailing + extend - masked
    return (factor, trailing)


def solution(mesh):
    placed = (
        P(("sub", "row", "col"), None),
        P(),
        P(("sub", "row"), "col"),
        P("sub", "col", "row"),
        P(),
        P(),
    )
    return jax.shard_map(
        per_device,
        mesh=mesh,
        in_specs=placed,
        out_specs=(P(("sub", "row", "col"), None), P(("sub", "row"), "col")),
        check_vma=False,
    )
```

profile of v0, /device:TPU:5, one launch (start us, length us, event | category | flops | bytes accessed | tf_op | source)
XLA Modules:
  0.0 1855.4 jit_solution(10755961113632533736)
XLA Ops:
  8.1 5.8 copy.17
  13.9 0.7 dynamic-slice_bitcast_fusion
  14.5 85.0 %all-gather.6.cloned.1.call-done = bf16[1,1280,5120]{1,2,0:T(8,128)(2,1)} async-done(((bf16[1,1280,1280]{1,2,0:T(8,128)(2,1)}), bf16[1,1280,5120]{1,2,0:T(8,128)(2,1)}) %all-gather.6.cloned.1.call-update) | async-done | bytes 13107216 | tf_op jit(solution)/shard_map/all_gather | solution.py:81
  99.6 21.1 %copy.18 = bf16[1280,20,256]{2,1,0:T(8,128)(2,1)} copy(bf16[1280,20,256]{0,2,1:T(8,128)(2,1)} %bitcast.60) | data formatting | bytes 26214400 | tf_op jit(solution)/shard_map/reshape | solution.py:34
  120.6 21.7 %convert_bitcast_fusion = bf16[1280,64,256]{2,1,0:T(8,128)(2,1)} fusion(bf16[1280,20,256]{2,1,0:T(8,128)(2,1)} %copy.18, s32[20]{0:T(128)S(1)} %dynamic-slice_bitcast_fusion), kind=kOutput, calls=%fused_computation.4 | convolution fusion | flops 859833600 | bytes 55050320 | tf_op jit(solution)/shard_map/rjt,jq->rqt/dot_general | solution.py:32
  142.3 68.0 %all_to_all.12 = bf16[1280,4,4096]{2,1,0:T(4,128)(2,1)} reshape(bf16[1280,64,256]{2,1,0:T(8,128)(2,1)} %convert_bitcast_fusion) | data formatting | bytes 83886080 | tf_op jit(solution)/shard_map/all_to_all | solution.py:83
  210.3 35.9 %copy.19 = bf16[1280,4,4096]{2,0,1:T(8,128)(2,1)} copy(bf16[1280,4,4096]{2,1,0:T(4,128)(2,1)} %all_to_all.12) | data formatting | bytes 83886080 | tf_op jit(solution)/shard_map/all_to_all | solution.py:83
  246.2 11.2 all-to-all-start
  257.4 0.0 all-gather.4.cloned.1.call-start
  257.5 4.6 copy.14
  262.2 0.0 all-reduce.3.cloned.1.call-start
  262.2 528.5 %all-gather.4.cloned.1.call-done = bf16[2048,3072]{0,1:T(8,128)(2,1)} async-done(((bf16[512,3072]{0,1:T(8,128)(2,1)}), bf16[2048,3072]{0,1:T(8,128)(2,1)}) %all-gather.4.cloned.1.call-update) | async-done | bytes 12582928 | tf_op jit(solution)/shard_map/all_gather | solution.py:68
  790.7 19.0 %bitcast_select_fusion = (bf16[2048,12,256]{0,2,1:T(8,128)(2,1)}, bf16[2048,12,256]{0,2,1:T(8,128)(2,1)}, bf16[12,256,2048]{2,1,0:T(8,128)(2,1)}) fusion(pred[]{:T(512)S(6)} %eq.57, pred[]{:T(512)S(6)} %eq.58, bf16[12,256,256]{2,1,0:T(8,128)(2,1)S(1)} %copy-done, bf16[2048,12,256]{0,2,1:T(8,128)(2,1)} %bitcast.63), kind=kOutput, calls=%fused_computation.11 | convolution fusion | flops 3240099840 | bytes 51904512 | tf_op jit(solution)/shard_map/rkt,kts->rks/dot_general | solution.py:23
  809.7 4.6 convolution_convert_fusion.1
  814.3 4.9 copy.30
  819.1 0.5 iota_add_fusion.1
  819.7 0.8 dynamic-slice_convert_fusion
  820.5 12.5 copy.38
  833.0 282.0 %all-reduce.3.cloned.1.call-done = (bf16[2048,3072]{0,1:T(8,128)(2,1)}, bf16[2048,3072]{0,1:T(8,128)(2,1)}) async-done(((bf16[2048,3072]{0,1:T(8,128)(2,1)}, bf16[2048,3072]{0,1:T(8,128)(2,1)}), (bf16[2048,3072]{0,1:T(8,128)(2,1)}, bf16[2048,3072]{0,1:T(8,128)(2,1)})) %all-reduce.3.cloned.1.call-update) | async-done | bytes 25165840 | tf_op jit(solution)/shard_map/psum | solution.py:9
  1115.0 20.6 %pad_maximum_fusion = bf16[4096,3072]{0,1:T(8,128)(2,1)} fusion(bf16[2048,3072]{0,1:T(8,128)(2,1)} %get-tuple-element.6, bf16[2048,3072]{0,1:T(8,128)(2,1)} %get-tuple-element.7), kind=kLoop, calls=%fused_computation.8 | loop fusion | flops 50331648 | bytes 50331648 | tf_op jit(solution)/shard_map/concatenate | solution.py:78
  1135.6 32.7 %copy.27 = bf16[4096,3072]{1,0:T(8,128)(2,1)} copy(bf16[4096,3072]{0,1:T(8,128)(2,1)} %pad_maximum_fusion) | data formatting | bytes 50331648 | tf_op jit(solution)/shard_map/concatenate | solution.py:78
  1168.3 193.4 %all-to-all-done = bf16[1280,4,4096]{2,0,1:T(8,128)(2,1)} async-done(((bf16[1280,4,4096]{2,0,1:T(8,128)(2,1)}), bf16[1280,4,4096]{2,0,1:T(8,128)(2,1)}, u32[]{:S(2)}, u32[]{:S(2)}) %all-to-all-start) | async-done | bytes 41943072 | tf_op jit(solution)/shard_map/all_to_all | solution.py:83
  1361.7 57.3 %fusion.7 = bf16[8,256,4096]{2,0,1:T(8,128)(2,1)} fusion(bf16[20,256,4096]{2,1,0:T(8,128)(2,1)} %bitcast.9, s32[20]{0:T(128)S(1)} %dynamic-slice_bitcast_fusion, s32[8]{0:T(128)S(1)} %iota_add_fusion), kind=kOutput, calls=%fused_computation.13 | convolution fusion | flops 343933088 | bytes 58720368 | tf_op jit(solution)/shard_map/itx,ip->ptx/dot_general | solution.py:46
  1419.0 18.5 copy.23
  1437.5 1.4 collective-permute-start
  1438.9 73.1 %convolution_multiply_fusion = f32[8,256,16,256]{3,1,2,0:T(8,128)} fusion(bf16[16,256,3072,1]{2,1,0,3:T(8,128)(2,1)} %bitcast.59, f32[8,16]{1,0:T(8,128)S(1)} %dynamic-slice_convert_fusion, bf16[8,256,3072,1]{1,0,2,3:T(8,128)(2,1)} %bitcast.61), kind=kOutput, calls=%fused_computation.9 | convolution fusion | flops 51547996160 | bytes 71303680 | tf_op jit(solution)/shard_map/dot_general | solution.py:94
  1512.0 28.4 %copy.29 = f32[8,256,16,256]{3,2,1,0:T(8,128)S(1)} copy(f32[8,256,16,256]{3,1,2,0:T(8,128)} %convolution_multiply_fusion) | data formatting | bytes 67108864 | tf_op jit(solution)/shard_map/mul | solution.py:99
  1540.4 36.3 %copy.39 = f32[256,8,16,256]{3,1,2,0:T(8,128)} copy(f32[256,8,16,256]{3,2,1,0:T(8,128)S(1)} %bitcast.53) | data formatting | bytes 67108864
  1576.7 58.4 %fusion.2 = f32[8,256,4096]{2,0,1:T(8,128)} fusion(bf16[20,256,4096]{2,1,0:T(8,128)(2,1)} %bitcast.9, s32[20]{0:T(128)S(1)} %dynamic-slice_bitcast_fusion, s32[8]{0:T(128)S(1)} %copy-done.2), kind=kOutput, calls=%fused_computation.2 | convolution fusion | flops 335544480 | bytes 75497584 | tf_op jit(solution)/shard_map/itx,ip->ptx/dot_general | solution.py:46
  1635.1 31.8 %copy.21 = f32[8,256,4096]{2,1,0:T(8,128)} copy(f32[8,256,4096]{2,0,1:T(8,128)} %fusion.2) | data formatting | bytes 67108864 | tf_op jit(solution)/shard_map/itx,ip->ptx/dot_general | solution.py:46
  1666.9 131.6 %collective-permute-done = bf16[2048,4096]{1,0:T(8,128)(2,1)} collective-permute-done((bf16[2048,4096]{1,0:T(8,128)(2,1)}, bf16[2048,4096]{1,0:T(8,128)(2,1)}, u32[]{:S(2)}, u32[]{:S(2)}) %collective-permute-start) | collective-permute-done | bytes 16777248 | tf_op jit(solution)/shard_map/ppermute | solution.py:15
  1798.5 49.0 %fusion.5 = f32[2048,4096]{1,0:T(8,128)} fusion(f32[2048,4096]{1,0:T(8,128)} %bitcast.54, f32[2048,4096]{1,0:T(8,128)} %param.8, f32[8,256,4096]{2,1,0:T(8,128)} %copy.21, bf16[2048,4096]{1,0:T(8,128)(2,1)} %collective-permute-done), kind=kLoop, calls=%fused_computation.7 | loop fusion | flops 33554432 | bytes 150994944 | tf_op jit(solution)/shard_map/sub | solution.py:101
  (11 shorter events, 0.1 us)
Async XLA Ops:
  8.0 782.7 %copy-start = (bf16[12,256,256]{2,1,0:T(8,128)(2,1)S(1)}, bf16[12,256,256]{2,1,0:T(8,128)(2,1)}, u32[]{:S(2)}) copy-start(bf16[12,256,256]{2,1,0:T(8,128)(2,1)} %param.7) | copy-start | bytes 4718596
  8.0 91.5 %all-gather.6.cloned.1.call-start = ((), (), s32[]{:S(2)}) async-start(), calls=%async_computation.2 | async-start | bytes 16384000 | tf_op jit(solution)/shard_map/all_gather | solution.py:81
  246.2 1115.5 %all-to-all-start = ((bf16[1280,4,4096]{2,0,1:T(8,128)(2,1)}), bf16[1280,4,4096]{2,0,1:T(8,128)(2,1)}, u32[]{:S(2)}, u32[]{:S(2)}) async-start(bf16[1280,4,4096]{2,0,1:T(8,128)(2,1)} %copy.19), calls=%async_computation | async-start | bytes 83886080 | tf_op jit(solution)/shard_map/all_to_all | solution.py:83
  257.4 533.3 %all-gather.4.cloned.1.call-start = ((), (), s32[]{:S(2)}) async-start(), calls=%async_computation.1 | async-start | bytes 15728640 | tf_op jit(solution)/shard_map/all_gather | solution.py:68
  262.2 852.8 %all-reduce.3.cloned.1.call-start = ((), (), s32[]{:S(2)}) async-start(), calls=%async_computation.3 | async-start | bytes 50331648 | tf_op jit(solution)/shard_map/psum | solution.py:9
  1437.5 361.0 %collective-permute-start = (bf16[2048,4096]{1,0:T(8,128)(2,1)}, bf16[2048,4096]{1,0:T(8,128)(2,1)}, u32[]{:S(2)}, u32[]{:S(2)}) collective-permute-start(bf16[2048,4096]{1,0:T(8,128)(2,1)} %bitcast.13), channel_id=1, source_target_pairs={{0,16},{16,0},{1,17},{17,1},{2,18},{18,2},{3,19},{19,3},{4,20},{20... | collective-permute-start | bytes 50331656 | tf_op jit(solution)/shard_map/ppermute | solution.py:15
  1540.4 36.3 %copy-start.2 = (s32[8]{0:T(128)S(1)}, s32[8]{0:T(128)}, u32[]{:S(2)}) copy-start(s32[8]{0:T(128)} %iota_add_fusion.1) | copy-start | bytes 100
  1798.5 49.0 %copy-start.1 = (bf16[12,256,256]{2,1,0:T(8,128)(2,1)S(1)}, bf16[12,256,256]{2,1,0:T(8,128)(2,1)}, u32[]{:S(2)}) copy-start(bf16[12,256,256]{2,1,0:T(8,128)(2,1)} %param.7) | copy-start | bytes 4718596
Sparse Core Ops, SparseCore 0:
  14.0 85.5 all-gather.5
Sparse Core Ops, SparseCore 1:
  262.2 528.4 all-gather.3
  809.8 305.1 all-reduce.2
where the time goes:
time: 1870 us; the launch traced here: 1860 us
  waiting for transfers between devices  1220 us (65%)
  local copies, waits for them, and re-layouts  301 us (16%)
  matrix products  234 us (13%)
  other arithmetic  71 us (4%)
    all_gather x1, waiting for transfers between devices, per_device(): front_rows = lax.all_gather(front_panel, 'col', axis=0, tiled=True)  528 us
    psum x1, waiting for transfers between devices, spread(): return lax.psum(kept, axis)  282 us
    all_to_all x1, waiting for transfers between devices, per_device(): lax.all_to_all(placed, 'col', split_axis=1, concat_axis=0, tiled=True)  193 us
    ppermute x1, waiting for transfers between devices, partner(): return lax.ppermute(value, axis, pairs)  132 us
    dot_general x2, matrix products, pick_rows(): jnp.einsum('itx,ip->ptx', child_block.reshape(tile_count, tile_size, widt...  116 us
    all_to_all x2, local copies, waits for them, and re-layouts, per_device(): lax.all_to_all(placed, 'col', split_axis=1, concat_axis=0, tiled=True)  104 us
    all_gather x1, waiting for transfers between devices, per_device(): gathered = lax.all_gather(own_child, 'row', axis=1, tiled=True)  85 us
    dot_general x1, matrix products, per_device(): lax.dot_general(row_panel, column_panel, (((1,), (1,)), ((), ())), prefer...  73.1 us
  transfers between devices with their start and end apart: 5, of which 5 were waited for; matrix products, arithmetic and copies ran while one was open for 18% of the time, Pallas kernels for 0%

commit v1 on v0

--- a/solution.py
+++ b/solution.py
@@ -1,7 +1,17 @@
+import functools
+import itertools
+
 import jax
 import jax.numpy as jnp
 from jax import lax
+from jax.experimental import pallas as pl
+from jax.experimental.pallas import tpu as pltpu
 from jax.sharding import PartitionSpec as P
+
+COL_WINDOW = 8
+ROW_WINDOWS = (14, 8, 6)
+CHUNKS = 6
+VMEM = 56 * 1024 * 1024
 
 
 def spread(value, axis, source):
@@ -52,7 +62,7 @@
     return picked.reshape(tile_rows * tile_size, width_cols)
 
 
-def per_device(front_panel, tile_inverse, front_trailing, child_update, child_map, pattern):
+def general_device(front_panel, tile_inverse, front_trailing, child_update, child_map, pattern):
     tile_size = tile_inverse.shape[1]
     parent_tiles = pattern.shape[0]
     block_rows = front_trailing.shape[0]
@@ -65,8 +75,7 @@
     rows_count = lax.axis_size("row")
     grid_row = sub_index * rows_count + row_index
     factor = apply_inverse(front_panel, tile_inverse)
-    front_rows = lax.all_gather(front_panel, "col", axis=0, tiled=True)
-    row_panel = apply_inverse(front_rows, tile_inverse)
+    row_panel = lax.all_gather(factor, "col", axis=0, tiled=True)
     share_rows = min(block_rows, block_cols)
     pieces = []
     for part_index in range(block_cols // share_rows):
@@ -102,6 +111,484 @@
     return (factor, trailing)
 
 
+def factor_kernel(panel_ref, inverse_ref, out_ref, *chunk_refs):
+    count, size, _ = inverse_ref.shape
+    per_chunk = count // len(chunk_refs)
+    for k in range(count):
+        here = (slice(None), pl.ds(k * size, size))
+        scaled = jnp.dot(
+            panel_ref[here], inverse_ref[k], preferred_element_type=jnp.float32
+        ).astype(out_ref.dtype)
+        out_ref[here] = scaled
+        chunk_refs[k // per_chunk][:, pl.ds(k % per_chunk * size, size)] = scaled
+
+
+def scale_panel(panel, inverses, chunks):
+    rows, depth = panel.shape
+    size = inverses.shape[1]
+    step, wide = rows // 4, depth // chunks
+    block = pl.BlockSpec((step, depth), lambda i: (i, 0))
+    shape = jax.ShapeDtypeStruct
+    return pl.pallas_call(
+        factor_kernel,
+        grid=(rows // step,),
+        in_specs=[block, pl.BlockSpec(inverses.shape, lambda i: (0, 0, 0))],
+        out_specs=[block] + [pl.BlockSpec((step, wide), lambda i: (i, 0))] * chunks,
+        out_shape=[shape(panel.shape, panel.dtype)] + [shape((rows, wide), panel.dtype)] * chunks,
+        compiler_params=pltpu.CompilerParams(vmem_limit_bytes=VMEM),
+        cost_estimate=pl.CostEstimate(
+            flops=2 * rows * depth * size, bytes_accessed=6 * panel.size, transcendentals=0
+        ),
+    )(panel, inverses)
+
+
+def extend_kernel(tile, parts, groups, order, count, row_at, col_at, me, base_ref, *refs):
+    strips, out_ref = refs[:-1], refs[-1]
+    i = pl.program_id(0)
+    part = tile // parts
+    window = col_at.shape[1] // groups
+
+    @pl.when((i == 0) | (i < count[0]))
+    def _():
+        out_ref[...] = base_ref[...]
+
+    for kid, group in itertools.product(range(2), range(groups)):
+
+        @pl.when((i < count[0]) & (row_at[kid * parts, order[i]] >= 0))
+        def _():
+            @pl.loop(0, window)
+            def _(b):
+                q = col_at[kid, group * window + b]
+
+                @pl.when(q >= 0)
+                def _():
+                    lanes = pl.ds(pl.multiple_of(q * tile, tile), tile)
+                    for m in range(parts):
+                        strip_ref = strips[(group * 2 + kid) * parts + m]
+                        first = pl.multiple_of((me[0] ^ m) * part, part)
+                        here = (pl.ds(first, part), lanes)
+                        out_ref[here] += strip_ref[0, b].astype(jnp.float32)
+
+
+def extend_add(base, strips, tables, me, tile):
+    height, width = base.shape
+    parts = tile // strips[0].shape[2]
+    groups = len(strips) // (2 * parts)
+    order, count, row_at, col_at = tables
+
+    def strip_spec(i):
+        return pl.BlockSpec(
+            (1,) + strips[i].shape[1:],
+            lambda p, order, count, row_at, *_: (
+                jnp.maximum(row_at[i % (2 * parts), order[p]], 0),
+                0,
+                0,
+                0,
+            ),
+        )
+
+    block = pl.BlockSpec((tile, width), lambda p, order, *_: (order[p], 0))
+    return pl.pallas_call(
+        functools.partial(extend_kernel, tile, parts, groups),
+        grid_spec=pltpu.PrefetchScalarGridSpec(
+            num_scalar_prefetch=5,
+            grid=(height // tile,),
+            in_specs=[block] + [strip_spec(i) for i in range(len(strips))],
+            out_specs=block,
+        ),
+        out_shape=jax.ShapeDtypeStruct(base.shape, base.dtype),
+        input_output_aliases={5: 0},
+        compiler_params=pltpu.CompilerParams(vmem_limit_bytes=VMEM),
+        cost_estimate=pl.CostEstimate(
+            flops=base.size, bytes_accessed=4 * base.size, transcendentals=0
+        ),
+    )(order, count.reshape(1), row_at, col_at, me.reshape(1), base, *strips)
+
+
+def update_kernel(tile, count, core, mask, *refs):
+    rows, mine, other = (refs[k * count : (k + 1) * count] for k in range(3))
+    base_ref, out_ref = refs[3 * count :]
+    i, c = pl.program_id(0), pl.program_id(1)
+    high, wide = out_ref.shape[0] // tile, out_ref.shape[1] // tile
+    per_side = pl.num_programs(1) // 2
+    first = column_block(c, per_side, core) * wide
+    for side, cols in enumerate((mine, other)):
+
+        @pl.when(c // per_side == side)
+        def _():
+            for q in range(wide):
+                lanes = pl.ds(q * tile, tile)
+                product = sum(
+                    lax.dot_general(
+                        rows_ref[...],
+                        cols_ref[lanes, :],
+                        (((1,), (1,)), ((), ())),
+                        preferred_element_type=jnp.float32,
+                    )
+                    for rows_ref, cols_ref in zip(rows, cols)
+                )
+                for a in range(high):
+                    here = (pl.ds(a * tile, tile), lanes)
+                    reached = mask[i * high + a, first + q].astype(jnp.float32)
+                    part = product[a * tile : (a + 1) * tile]
+                    out_ref[here] = base_ref[here] - reached * part
+
+
+def column_block(c, per_side, core):
+    return (c // per_side ^ core[0]) * per_side + c % per_side
+
+
+def update(base, rows, mine, other, mask, core, tile, in_place):
+    height, width = base.shape
+    step = 4 * tile
+    per_side = width // step // 2
+    block = pl.BlockSpec((step, step), lambda i, c, core, _: (i, column_block(c, per_side, core)))
+    row_block = lambda i, c, *_: (i, 0)
+    mine_block = lambda i, c, *_: (jnp.minimum(c, per_side - 1), 0)
+    other_block = lambda i, c, *_: (jnp.maximum(c - per_side, 0), 0)
+    specs = [
+        pl.BlockSpec((step, piece.shape[1]), at)
+        for pieces, at in ((rows, row_block), (mine, mine_block), (other, other_block))
+        for piece in pieces
+    ]
+    depth = sum(piece.shape[1] for piece in rows)
+    return pl.pallas_call(
+        functools.partial(update_kernel, tile, len(rows)),
+        grid_spec=pltpu.PrefetchScalarGridSpec(
+            num_scalar_prefetch=2,
+            grid=(height // step, width // step),
+            in_specs=specs + [block],
+            out_specs=block,
+        ),
+        out_shape=jax.ShapeDtypeStruct(base.shape, base.dtype),
+        input_output_aliases={2 + 3 * len(rows): 0} if in_place else {},
+        compiler_params=pltpu.CompilerParams(vmem_limit_bytes=VMEM),
+        cost_estimate=pl.CostEstimate(
+            flops=2 * height * width * depth, bytes_accessed=8 * base.size, transcendentals=0
+        ),
+    )(core.reshape(1), mask, *rows, *mine, *other, base)
+
+
+def xor_permute(value, axes, size, mask):
+    if mask == 0:
+        return value
+    return lax.ppermute(value, axes, [(i, i ^ mask) for i in range(size)])
+
+
+def line_device(front_panel, tile_inverse, front_trailing, child_update, child_map, pattern):
+    tile = tile_inverse.shape[1]
+    block_rows, block_cols = front_trailing.shape
+    tile_rows, tile_cols = block_rows // tile, block_cols // tile
+    subs, rows, planes = (lax.axis_size(name) for name in ("sub", "row", "col"))
+    grid = subs * rows
+    cores = 2
+    plane_axes = ("sub", "row")
+    s, r, z = (lax.axis_index(name) for name in ("sub", "row", "col"))
+    grid_row = s * rows + r
+    chip, core = grid_row // cores, grid_row % cores
+    shard = front_panel.shape[0]
+
+    factor, *chunks = scale_panel(front_panel, tile_inverse, CHUNKS)
+
+    child = child_update[0]
+    own_rows, own_cols = child.shape[0] // tile, child.shape[1] // tile
+    child_tiles = child_map.shape[1]
+    part = tile // rows
+    col_window = min(COL_WINDOW, child_tiles)
+    row_windows = [min(size, child_tiles) for size in ROW_WINDOWS]
+
+    def send_strips():
+        shaped = child.reshape(own_rows, rows, part, own_cols, tile).transpose(1, 0, 3, 2, 4)
+        return [
+            xor_permute(
+                lax.dynamic_index_in_dim(shaped, r ^ m, 0, keepdims=False), "row", rows, m
+            )
+            for m in range(rows)
+        ]
+
+    def edges_of(count):
+        first = jnp.arange(count + 1, dtype=jnp.int32) * (pattern.shape[0] // count)
+        return (child_map[:, None, :] < first[None, :, None]).sum(-1, dtype=jnp.int32)
+
+    def rounds_of(edges, size):
+        return (jnp.max(edges[:, 1:] - edges[:, :-1]) + size - 1) // size
+
+    col_edges = edges_of(planes)
+    row_edges = [edges_of(count) for count in (subs, subs * rows // cores, grid)]
+    rounds = [rounds_of(col_edges, col_window)]
+    rounds += [rounds_of(edges, size) for edges, size in zip(row_edges, row_windows)]
+
+    def turns_of(turn):
+        turns = []
+        for count in reversed(rounds):
+            turns.append(turn % count)
+            turn = turn // count
+        return turns[::-1]
+
+    def col_start(kid, plane, turn):
+        return jnp.minimum(col_edges[kid, plane] + turn * col_window, child_tiles - col_window)
+
+    def row_starts(kid, row, turns):
+        start, size, found = 0, child_tiles, []
+        places_at = (row // rows, row // cores, row)
+        for edges, at, turn, window in zip(row_edges, places_at, turns, row_windows):
+            start = jnp.clip(edges[kid, at] + turn * window, start, start + size - window)
+            size = window
+            found.append(start)
+        return found
+
+    def send_columns(strips, turn):
+        stripped = jnp.zeros((own_rows, child_tiles, part, tile), child.dtype)
+        for m, got in enumerate(strips):
+            stripped = lax.dynamic_update_slice(stripped, got, (0, (r ^ m) * own_cols, 0, 0))
+        pieces = []
+        for m in range(planes):
+            start = col_start(s, z ^ m, turn)
+            piece = lax.dynamic_slice_in_dim(stripped, start, col_window, 1)
+            pieces.append(xor_permute(piece, "col", planes, m))
+        return pieces
+
+    def join_columns(pieces):
+        groups = []
+        for half in range(2):
+            placed = jnp.zeros((child_tiles, col_window // 2, part, tile), child.dtype)
+            for m, got in enumerate(pieces):
+                got = got[:, half * col_window // 2 : (half + 1) * col_window // 2]
+                placed = lax.dynamic_update_slice(placed, got, ((z ^ m) * own_rows, 0, 0, 0))
+            groups.append(placed)
+        return groups
+
+    def taken(value, start, size):
+        return lax.dynamic_slice_in_dim(value, start, size, 0)
+
+    kids = (s, 1 - s)
+
+    size = row_windows[1]
+
+    def rows_for(values, row, turns, level=None):
+        parts = []
+        for value, kid in zip(values, kids):
+            found = row_starts(kid, row, turns)
+            first = 0 if level is None else found[level]
+            parts.append(taken(value, found[1] - first, size))
+        return parts
+
+    def halves_first(placed, turns):
+        here, there = (row_starts(s, row, turns)[0] for row in (grid_row, grid_row ^ rows))
+        window = row_windows[0]
+        return [
+            taken(placed, here, window),
+            xor_permute(taken(placed, there, window), "sub", subs, 1),
+        ]
+
+    def chips_second(halves, turns):
+        here, there = (
+            jnp.concatenate(rows_for(halves, row, turns, 0), axis=0)
+            for row in (grid_row, grid_row ^ cores)
+        )
+        return [here, xor_permute(there, "row", rows, cores)]
+
+    def chips_first(placed, turns):
+        def of_both_halves(row):
+            found = [rows_for([placed], half * rows + row, turns)[0] for half in range(subs)]
+            return jnp.concatenate(found, axis=0)
+
+        return [of_both_halves(r), xor_permute(of_both_halves(r ^ cores), "row", rows, cores)]
+
+    def halves_second(strips, turns):
+        here, there = (
+            [taken(strip, half * size, size) for strip in strips] for half in kids
+        )
+        got = xor_permute(jnp.concatenate(there, axis=0), "sub", subs, 1)
+        return [
+            jnp.concatenate((kept, got[k * size : (k + 1) * size]), axis=0)
+            for k, kept in enumerate(here)
+        ]
+
+    def send_cores(strips, turns):
+        found = [row_starts(kid, grid_row ^ 1, turns) for kid in kids]
+        parts = [
+            taken(strip, kid * size + at[2] - at[1], row_windows[2])
+            for strip in strips
+            for kid, at in enumerate(found)
+        ]
+        return xor_permute(jnp.concatenate(parts, axis=0), "row", rows, 1)
+
+    def tables_of(turns):
+        col_turn, row_turns = turns[0], turns[1:]
+        col_at, row_at = [], []
+        wanted = grid_row * tile_rows + jnp.arange(tile_rows, dtype=jnp.int32)
+        for place, kid in enumerate(kids):
+            own_map = lax.dynamic_index_in_dim(child_map, kid, 0, keepdims=False)
+            first = col_edges[kid, z] + col_turn * col_window
+            last = jnp.minimum(first + col_window, col_edges[kid, z + 1])
+            start = col_start(kid, z, col_turn)
+            slot = start + jnp.arange(col_window, dtype=jnp.int32)
+            parent = lax.dynamic_slice_in_dim(own_map, start, col_window) - z * tile_cols
+            col_at.append(jnp.where((slot >= first) & (slot < last), parent, -1))
+
+            same = own_map[None, :] == wanted[:, None]
+            slot = jnp.max(jnp.where(same, jnp.arange(child_tiles, dtype=jnp.int32), -1), axis=1)
+            held = slot >= 0
+            at_level = (s, chip, grid_row)
+            for edges, at, turn, window in zip(row_edges, at_level, row_turns, row_windows):
+                first = edges[kid, at] + turn * window
+                held &= (slot >= first) & (slot < first + window)
+            starts = row_starts(kid, grid_row, row_turns)
+            near_at = place * row_windows[1] + slot - starts[1]
+            far_at = [(k * 2 + place) * row_windows[2] + slot - starts[2] for k in range(2)]
+            order = (near_at, far_at[0], near_at, far_at[1])
+            row_at += [jnp.where(held, at, -1) for at in order]
+        row_at, col_at = jnp.stack(row_at), jnp.stack(col_at)
+        reached = jnp.max(row_at, axis=0) >= 0
+        count = jnp.sum(reached, dtype=jnp.int32)
+        every = jnp.arange(tile_rows, dtype=jnp.int32)
+        before = jnp.sum(reached[None, :] & (every[None, :] < every[:, None]), axis=1, dtype=jnp.int32)
+        wanted = jnp.minimum(every, jnp.maximum(count - 1, 0))
+        listed = reached[None, :] & (before[None, :] == wanted[:, None])
+        order = jnp.max(jnp.where(listed, every[None, :], 0), axis=1)
+        return order, count, row_at, col_at
+
+    def extend(base, near, far, tables):
+        strips = [strip for (a, b), c in zip(near, far) for strip in (a, c, b, c) * 2]
+        return extend_add(base, strips, tables, r, tile)
+
+    fence = lax.optimization_barrier
+    chunks, child = fence((chunks, child))
+
+    def gather(pieces):
+        return [lax.all_gather(piece, "col", axis=0, tiled=True) for piece in pieces]
+
+    row_chunks = gather(chunks[:1])
+
+    ring = ((0, 2, 3, 1), (0, 1, 3, 2))
+    place = chip ^ z
+    half = block_rows // 2
+
+    def device_at(c, k, plane):
+        return (c * cores + k) * planes + plane
+
+    def hand_on(held, hops):
+        pairs = [
+            (device_at(p ^ a, k, p), device_at(p ^ b, k, p))
+            for a, b in hops
+            for p in range(planes)
+            for k in range(cores)
+        ]
+        return lax.ppermute(held, ("sub", "row", "col"), pairs)
+
+    def halves_of(c):
+        return row_chunks[c][:half], row_chunks[c][half:]
+
+    def beat(at, got):
+        taken_on = []
+        for side, way in enumerate(ring):
+            hops = [(way[h], way[h + 1]) for h in range(3) if 0 <= at - h < CHUNKS]
+            if at < CHUNKS:
+                held = halves_of(at)[side]
+                if at > 0:
+                    held = jnp.where(place == 0, held, got[at - 1][side])
+            else:
+                held = got[at - 1][side]
+            taken_on.append(hand_on(held, hops))
+        return got + [taken_on]
+
+    def columns_of(c, got, straight=None):
+        halves = []
+        for side, (held, way) in enumerate(zip(halves_of(c), ring)):
+            found = [got[c][side], got[c + 1][side]]
+            found.append(got[c + 2][side] if straight is None else straight[side])
+            for target, value in zip(way[1:], found):
+                held = jnp.where(place == target, value, held)
+            halves.append(held)
+        mine = jnp.concatenate(halves, axis=0)
+        return mine, xor_permute(mine, "row", rows, 1)
+
+    local_mask = lax.dynamic_slice(
+        pattern, (grid_row * tile_rows, z * tile_cols), (tile_rows, tile_cols)
+    )
+
+    def subtract(base, first, columns, in_place=True):
+        mine, other = zip(*columns)
+        part = row_chunks[first : first + len(columns)]
+        return update(base, part, mine, other, local_mask, core, tile, in_place)
+
+    no_turns = [0] * 4
+    row_turns = no_turns[1:]
+    strips = fence(send_strips())
+
+    got = beat(0, [])
+    pieces = send_columns(strips, 0)
+    tables = tables_of(no_turns)
+    got, pieces, chunks, tables, local_mask = fence((got, pieces, chunks, tables, local_mask))
+    row_chunks = row_chunks + gather(chunks[1:])
+
+    def first_rows(placed, turns):
+        return halves_first(placed[0], turns), chips_first(placed[1], turns)
+
+    def second_rows(first, turns):
+        return chips_second(first[0], turns), halves_second(first[1], turns)
+
+    def third_rows(near, turns):
+        return [send_cores(group, turns) for group in near]
+
+    halfway = fence(first_rows(join_columns(pieces), row_turns))
+
+    near = second_rows(halfway, row_turns)
+    got = beat(1, got)
+    got, near = fence((got, near))
+
+    far = third_rows(near, row_turns)
+    got = beat(2, got)
+    got, far = fence((got, far))
+
+    columns = [columns_of(0, got)]
+    base = subtract(front_trailing, 0, columns, False)
+    got = beat(3, got)
+    got, base = fence((got, base))
+
+    columns.append(columns_of(1, got))
+    base = extend(base, near, far, tables)
+    got = beat(4, got)
+    got, base, columns = fence((got, base, columns))
+
+    columns.append(columns_of(2, got))
+    base = subtract(base, 1, columns[1:2])
+    got = beat(5, got)
+    got, base, columns = fence((got, base, columns))
+
+    columns.append(columns_of(3, got))
+    straight = [hand_on(held, [(0, way[3])]) for held, way in zip(halves_of(5), ring)]
+    got = beat(6, got)
+
+    def more(turn, base):
+        turns = turns_of(turn)
+        placed = join_columns(send_columns(strips, turns[0]))
+        near = second_rows(first_rows(placed, turns[1:]), turns[1:])
+        return extend(base, near, third_rows(near, turns[1:]), tables_of(turns))
+
+    every_round = functools.reduce(lambda a, b: a * b, rounds)
+    base = lax.fori_loop(1, every_round, more, base)
+    base = subtract(base, 2, columns[2:])
+    base, got, straight = fence((base, got, straight))
+    base = subtract(base, 4, [columns_of(4, got), columns_of(5, got, straight)])
+    return (factor, base)
+
+
+def fits_line(mesh, front_trailing, child_update, tile):
+    sizes = [mesh.shape[name] for name in ("sub", "row", "col")]
+    grid = sizes[0] * sizes[1]
+    block_rows = front_trailing.shape[0] // grid
+    block_cols = front_trailing.shape[1] // sizes[2]
+    child_parts = (child_update.shape[1] // sizes[2], child_update.shape[2] // sizes[1])
+    return (
+        sizes == [2, 4, 4]
+        and block_cols == 2 * block_rows
+        and all(part % tile == 0 for part in child_parts)
+        and block_rows % (4 * 2 * tile) == 0
+    )
+
+
 def solution(mesh):
     placed = (
         P(("sub", "row", "col"), None),
@@ -111,10 +598,15 @@
         P(),
         P(),
     )
-    return jax.shard_map(
-        per_device,
-        mesh=mesh,
-        in_specs=placed,
-        out_specs=(P(("sub", "row", "col"), None), P(("sub", "row"), "col")),
-        check_vma=False,
-    )
+
+    def whole(front_panel, tile_inverse, front_trailing, child_update, child_map, pattern):
+        on_line = fits_line(mesh, front_trailing, child_update, tile_inverse.shape[1])
+        return jax.shard_map(
+            line_device if on_line else general_device,
+            mesh=mesh,
+            in_specs=placed,
+            out_specs=(P(("sub", "row", "col"), None), P(("sub", "row"), "col")),
+            check_vma=False,
+        )(front_panel, tile_inverse, front_trailing, child_update, child_map, pattern)
+
+    return whole

time: 1870 us -> 596 us (0.32)
  waiting for transfers between devices: 1220 us -> 240 us
  local copies, waits for them, and re-layouts: 301 us -> 46.3 us
  matrix products: 234 us -> 0 us
  Pallas kernels: 0 us -> 157 us
  starting transfers between devices: 12.8 us -> 51.4 us
  between operations: 16 us -> 43.4 us
  other arithmetic: 71 us -> 47.8 us
    all_gather x2 -> x6, waiting for transfers between devices: 613 us -> 0.04 us  [gather(): lax.all_gather(piece, 'col', axis=0, tiled=True)]
    psum x1 -> x0, waiting for transfers between devices: 282 us -> none  [spread(): return lax.psum(kept, axis)]
    dot_general x6 -> x0, matrix products: 234 us -> none  [the longest x2 116 us: pick_rows(): jnp.einsum('itx,ip->ptx', child_block.reshape(tile_count, tile_size, widt...]
    all_to_all x1 -> x0, waiting for transfers between devices: 193 us -> none  [per_device(): lax.all_to_all(placed, 'col', split_axis=1, concat_axis=0, tiled=True)]
    pallas_call x0 -> x6, Pallas kernels: none -> 157 us  [the longest x4 129 us: update(): pl.pallas_call(functools.partial(update_kernel, tile, len(rows)), grid_sp...]
    ppermute x1 -> x34, waiting for transfers between devices: 132 us -> 240 us  [the longest x18 184 us: xor_permute(): return lax.ppermute(value, axes, [(i, i ^ mask) for i in range(size)])]
    all_to_all x2 -> x0, local copies, waits for them, and re-layouts: 104 us -> none  [per_device(): lax.all_to_all(placed, 'col', split_axis=1, concat_axis=0, tiled=True)]
    unnamed x11 -> x74, local copies, waits for them, and re-layouts: 64.2 us -> 8.19 us
  transfers between devices with their start and end apart: 5 -> 40, of which waited for: 5 -> 14; matrix products, arithmetic and copies ran while one was open for 18% -> 14% of each run, Pallas kernels for 0% -> 20%
where the time goes in v1:
time: 596 us; the launch traced here: 586 us
  waiting for transfers between devices  240 us (40%)
  Pallas kernels  157 us (26%)
  starting transfers between devices  51.4 us (9%)
  other arithmetic  47.8 us (8%)
  local copies, waits for them, and re-layouts  46.3 us (8%)
  between operations  43.4 us (7%)
    ppermute x18, waiting for transfers between devices, xor_permute(): return lax.ppermute(value, axes, [(i, i ^ mask) for i in range(size)])  184 us
    pallas_call x4, Pallas kernels, update(): pl.pallas_call(functools.partial(update_kernel, tile, len(rows)), grid_sp...  129 us
    ppermute x16, waiting for transfers between devices, hand_on(): return lax.ppermute(held, ('sub', 'row', 'col'), pairs)  55.7 us
    ppermute x16, starting transfers between devices, hand_on(): return lax.ppermute(held, ('sub', 'row', 'col'), pairs)  33.8 us
    pallas_call x1, Pallas kernels, extend_add(): pl.pallas_call(functools.partial(extend_kernel, tile, parts, groups), gri...  22.1 us
    ppermute x18, starting transfers between devices, xor_permute(): return lax.ppermute(value, axes, [(i, i ^ mask) for i in range(size)])  17.4 us
    select_n x4, other arithmetic, beat(): held = jnp.where(place == 0, held, got[at - 1][side])  15.9 us
  transfers between devices with their start and end apart: 40, of which 14 were waited for; matrix products, arithmetic and copies ran while one was open for 14% of the time, Pallas kernels for 20%

profile of v1, /device:TPU:5, one launch (start us, length us, event | category | flops | bytes accessed | tf_op | source)
XLA Modules:
  0.0 585.8 jit_solution(5271560860725303820)
XLA Ops:
  7.2 6.0 %shard_map.77 = (bf16[512,3072]{1,0:T(8,128)(2,1)}, bf16[512,512]{1,0:T(8,128)(2,1)}, bf16[512,512]{1,0:T(8,128)(2,1)}, bf16[512,512]{1,0:T(8,128)(2,1)}, bf16[5...) custom-call(bf16[512,3072]{1,0:T(8,128)(2,1)} %panel_ref.1, bf16[12,256,256]{2,1,0:T(8,128)(2,1)} %inverse_ref.1), custom_call_target="tpu_custom_call" | custom-call | flops 805306368 | bytes 9437184 | tf_op jit(solution)/shard_map/pallas_call | solution.py:132
  13.3 5.6 reshape.731
  18.9 3.9 constant_dynamic-slice_fusion.44
  34.1 11.8 %collective-permute-done.12 = bf16[5,5,64,256]{3,2,1,0:T(8,128)(2,1)S(1)} collective-permute-done((bf16[5,5,64,256]{3,2,1,0:T(8,128)(2,1)}, bf16[5,5,64,256]{3,2,1,0:T(8,128)(2,1)S(1)}, u32[]{:S(2)}, u32[]{:S(2)}) %collective-permute-start.12) | collective-permute-done | bytes 819232 | tf_op jit(solution)/shard_map/ppermute | solution.py:275
  45.9 17.5 %collective-permute-done.13 = bf16[5,5,64,256]{3,2,1,0:T(8,128)(2,1)S(1)} collective-permute-done((bf16[5,5,64,256]{3,2,1,0:T(8,128)(2,1)}, bf16[5,5,64,256]{3,2,1,0:T(8,128)(2,1)S(1)}, u32[]{:S(2)}, u32[]{:S(2)}) %collective-permute-start.13) | collective-permute-done | bytes 819232 | tf_op jit(solution)/shard_map/ppermute | solution.py:275
  66.5 3.4 collective-permute-start.16
  70.2 3.0 fusion.29
  86.4 3.7 fusion.22
  99.0 83.2 %collective-permute-done.15 = bf16[5,8,64,256]{3,2,1,0:T(8,128)(2,1)} collective-permute-done((bf16[5,8,64,256]{3,2,1,0:T(8,128)(2,1)}, bf16[5,8,64,256]{3,2,1,0:T(8,128)(2,1)}, u32[]{:S(2)}, u32[]{:S(2)}) %collective-permute-start.15) | collective-permute-done | bytes 1310752 | tf_op jit(solution)/shard_map/ppermute | solution.py:275
  200.8 37.8 %collective-permute-done.19 = bf16[14,4,64,256]{3,2,1,0:T(8,128)(2,1)} collective-permute-done((bf16[14,4,64,256]{3,2,1,0:T(8,128)(2,1)}, bf16[14,4,64,256]{3,2,1,0:T(8,128)(2,1)}, u32[]{:S(2)}, u32[]{:S(2)}) %collective-permute-start.19) | collective-permute-done | bytes 1835040 | tf_op jit(solution)/shard_map/ppermute | solution.py:275
  238.6 3.2 collective-permute-done.20
  243.1 2.8 constant_dynamic-slice_fusion.24
  252.2 2.8 constant_dynamic-slice_fusion.28
  256.6 3.4 broadcast_select_fusion.8
  269.6 23.0 %collective-permute-done.22 = bf16[16,4,64,256]{3,2,1,0:T(8,128)(2,1)} collective-permute-done((bf16[16,4,64,256]{3,2,1,0:T(8,128)(2,1)}, bf16[16,4,64,256]{3,2,1,0:T(8,128)(2,1)}, u32[]{:S(2)}, u32[]{:S(2)}) %collective-permute-start.22) | collective-permute-done | bytes 2097184 | tf_op jit(solution)/shard_map/ppermute | solution.py:275
  296.1 27.7 %collective-permute-done.18 = bf16[1024,512]{1,0:T(8,128)(2,1)S(1)} collective-permute-done((bf16[1024,512]{1,0:T(8,128)(2,1)}, bf16[1024,512]{1,0:T(8,128)(2,1)S(1)}, u32[]{:S(2)}, u32[]{:S(2)}) %collective-permute-start.18) | collective-permute-done | bytes 1048608 | tf_op jit(solution)/shard_map/ppermute | solution.py:478
  327.7 3.4 collective-permute-start.26
  332.9 3.7 broadcast_select_fusion.6
  340.0 22.9 %collective-permute-done.24 = bf16[1024,512]{1,0:T(8,128)(2,1)} collective-permute-done((bf16[1024,512]{1,0:T(8,128)(2,1)}, bf16[1024,512]{1,0:T(8,128)(2,1)}, u32[]{:S(2)}, u32[]{:S(2)}) %collective-permute-start.24) | collective-permute-done | bytes 1048608 | tf_op jit(solution)/shard_map/ppermute | solution.py:478
  364.8 5.4 broadcast_select_fusion.4
  376.1 29.2 %shard_map.78.base_ref = f32[2048,4096]{1,0:T(8,128)} custom-call(s32[1]{0:T(128)} %bitcast.44.core, s32[8,16]{1,0:T(8,128)} %dynamic_slice.726.mask, bf16[2048,512]{1,0:T(8,128)(2,1)} %all-gather.7.cloned.1.call-done.refs_0_, bf16[2048,512]{1,0:T(8,128)(2,1)} %copy-done.37, bf16[2048,512]{1,0:T(8,128)(2,1)} %collective-permute-done.29.refs_2_, ...), custom_call_target="tpu_custom_call" | custom-call | flops 8589934592 | bytes 67108864 | tf_op jit(solution)/shard_map/pallas_call | solution.py:255
  405.3 3.4 broadcast_select_fusion.2
  409.3 4.7 collective-permute-start.31
  415.2 22.1 %shard_map.79.refs_3_ = f32[2048,4096]{1,0:T(8,128)} custom-call(s32[8]{0:T(128)} %select_reduce_fusion.3.order, s32[1]{0:T(128)} %bitcast.90.count, s32[8,8]{1,0:T(8,128)} %stack.16.row_at, s32[2,8]{1,0:T(2,128)} %pad_add_fusion.1.col_at, s32[1]{0:T(128)} %bitcast.91.me, f32[2048,4096]{1,0:T(8,128)} %shard_map.78.base_ref, ...), custom_call_target="tpu_custom_call", output_to_operand_aliasing={{}: (5, {})} | custom-call | flops 8388608 | bytes 33554432 | tf_op jit(solution)/shard_map/pallas_call | solution.py:191
  437.4 3.2 collective-permute-done.30
  440.6 3.7 fusion.27
  446.9 4.0 collective-permute-start.34
  456.7 28.9 %shard_map.80 = f32[2048,4096]{1,0:T(8,128)} custom-call(s32[1]{0:T(128)} %bitcast.44.core, s32[8,16]{1,0:T(8,128)} %dynamic_slice.726.mask, bf16[2048,512]{1,0:T(8,128)(2,1)} %all-gather.17.cloned.1.call-done.refs_0_, bf16[2048,512]{1,0:T(8,128)(2,1)} %copy-done.36, ...), custom_call_target="tpu_custom_call", output_to_operand_aliasing={{}: (5, {})} | custom-call | flops 8589934592 | bytes 67108864 | tf_op jit(solution)/shard_map/pallas_call | solution.py:255
  492.5 5.2 collective-permute-start.38
  497.8 35.7 %shard_map.81.refs_6_ = f32[2048,4096]{1,0:T(8,128)} custom-call(s32[1]{0:T(128)} %bitcast.44.core, s32[8,16]{1,0:T(8,128)} %dynamic_slice.726.mask, bf16[2048,512]{1,0:T(8,128)(2,1)} %all-gather.13.cloned.1.call-done.refs_0_, bf16[2048,512]{1,0:T(8,128)(2,1)} %all-gather.15.cloned.1.call-done.refs_1_, ...), custom_call_target="tpu_custom_call", output_to_operand_aliasing={{}: (8, {})} | custom-call | flops 17179869184 | bytes 67108864 | tf_op jit(solution)/shard_map/pallas_call | solution.py:255
  540.3 3.1 collective-permute-done.42.refs_5_
  543.4 35.1 %shard_map.82 = f32[2048,4096]{1,0:T(8,128)} custom-call(s32[1]{0:T(128)} %bitcast.44.core, s32[8,16]{1,0:T(8,128)} %dynamic_slice.726.mask, bf16[2048,512]{1,0:T(8,128)(2,1)} %all-gather.9.cloned.1.call-done.refs_0_, bf16[2048,512]{1,0:T(8,128)(2,1)} %all-gather.11.cloned.1.call-done.refs_1_, ...), custom_call_target="tpu_custom_call", output_to_operand_aliasing={{}: (8, {})} | custom-call | flops 17179869184 | bytes 67108864 | tf_op jit(solution)/shard_map/pallas_call | solution.py:255
  (208 shorter events, 90.1 us)
Async XLA Ops:
  7.2 63.0 %all-gather.7.cloned.1.call-start = ((), (), s32[]{:S(2)}) async-start(), calls=%async_computation | async-start | bytes 2621440 | tf_op jit(solution)/shard_map/all_gather | solution.py:460
  13.2 243.4 %all-gather.17.cloned.1.call-start = ((), (), s32[]{:S(2)}) async-start(), calls=%async_computation.5 | async-start | bytes 2621440 | tf_op jit(solution)/shard_map/all_gather | solution.py:460
  26.8 36.6 %collective-permute-start.13 = (bf16[5,5,64,256]{3,2,1,0:T(8,128)(2,1)}, bf16[5,5,64,256]{3,2,1,0:T(8,128)(2,1)S(1)}, u32[]{:S(2)}, u32[]{:S(2)}) collective-permute-start(bf16[5,5,64,256]{3,2,1,0:T(8,128)(2,1)} %bitcast.146), channel_id=1, source_target_pairs={{0,12},{4,8},{8,4},{12,0},{1,13},{5,9},{9,5},{13,1},{2,14},{6,10},... | collective-permute-start | bytes 2457608 | tf_op jit(solution)/shard_map/ppermute | solution.py:275
  66.5 32.5 %collective-permute-start.16 = (bf16[5,8,64,256]{3,2,1,0:T(8,128)(2,1)}, bf16[5,8,64,256]{3,2,1,0:T(8,128)(2,1)}, u32[]{:S(2)}, u32[]{:S(2)}) collective-permute-start(bf16[5,8,64,256]{3,2,1,0:T(8,128)(2,1)} %get-tuple-element.2850), channel_id=1, source_target_pairs={{0,3},{1,2},{2,1},{3,0},{4,7},{5,6},{6,5},{7,4},{8,11},{9,10},{10,... | collective-permute-start | bytes 3932168 | tf_op jit(solution)/shard_map/ppermute | solution.py:275
  69.9 112.3 %collective-permute-start.15 = (bf16[5,8,64,256]{3,2,1,0:T(8,128)(2,1)}, bf16[5,8,64,256]{3,2,1,0:T(8,128)(2,1)}, u32[]{:S(2)}, u32[]{:S(2)}) collective-permute-start(bf16[5,8,64,256]{3,2,1,0:T(8,128)(2,1)} %get-tuple-element.2851), channel_id=1, source_target_pairs={{0,2},{1,3},{2,0},{3,1},{4,6},{5,7},{6,4},{7,5},{8,10},{9,11},{10,... | collective-permute-start | bytes 3932168 | tf_op jit(solution)/shard_map/ppermute | solution.py:275
  69.9 112.3 %collective-permute-start.14 = (bf16[5,8,64,256]{3,2,1,0:T(8,128)(2,1)}, bf16[5,8,64,256]{3,2,1,0:T(8,128)(2,1)}, u32[]{:S(2)}, u32[]{:S(2)}) collective-permute-start(bf16[5,8,64,256]{3,2,1,0:T(8,128)(2,1)} %get-tuple-element.2852), channel_id=1, source_target_pairs={{0,1},{1,0},{2,3},{3,2},{4,5},{5,4},{6,7},{7,6},{8,9},{9,8},{10,11... | collective-permute-start | bytes 3932168 | tf_op jit(solution)/shard_map/ppermute | solution.py:275
  73.2 109.0 %collective-permute-start.10 = (bf16[1024,512]{1,0:T(8,128)(2,1)}, bf16[1024,512]{1,0:T(8,128)(2,1)S(1)}, u32[]{:S(2)}, u32[]{:S(2)}) collective-permute-start(bf16[1024,512]{1,0:T(8,128)(2,1)} %get-tuple-element.2902), channel_id=1, source_target_pairs={{0,8},{4,12},{9,1},{13,5},{18,26},{22,30},{27,19},{31,23}} | collective-permute-start | bytes 3145736 | tf_op jit(solution)/shard_map/ppermute | solution.py:478
  74.5 107.7 %collective-permute-start.9 = (bf16[1024,512]{1,0:T(8,128)(2,1)}, bf16[1024,512]{1,0:T(8,128)(2,1)S(1)}, u32[]{:S(2)}, u32[]{:S(2)}) collective-permute-start(bf16[1024,512]{1,0:T(8,128)(2,1)} %get-tuple-element.2903), channel_id=1, source_target_pairs={{0,16},{4,20},{9,25},{13,29},{18,2},{22,6},{27,11},{31,15}} | collective-permute-start | bytes 3145736 | tf_op jit(solution)/shard_map/ppermute | solution.py:478
  182.2 150.6 %all-gather.13.cloned.1.call-start = ((), (), s32[]{:S(2)}) async-start(), calls=%async_computation.3 | async-start | bytes 2621440 | tf_op jit(solution)/shard_map/all_gather | solution.py:460
  195.6 46.2 %collective-permute-start.20 = (bf16[16,4,64,256]{3,2,1,0:T(8,128)(2,1)}, bf16[16,4,64,256]{3,2,1,0:T(8,128)(2,1)}, u32[]{:S(2)}, u32[]{:S(2)}) collective-permute-start(bf16[16,4,64,256]{3,2,1,0:T(8,128)(2,1)} %pad_maximum_fusion.11), channel_id=1, source_target_pairs={{0,8},{4,12},{8,0},{12,4},{1,9},{5,13},{9,1},{13,5},{2,10},{6,14},... | collective-permute-start | bytes 6291464 | tf_op jit(solution)/shard_map/ppermute | solution.py:275
  198.2 40.4 %collective-permute-start.19 = (bf16[14,4,64,256]{3,2,1,0:T(8,128)(2,1)}, bf16[14,4,64,256]{3,2,1,0:T(8,128)(2,1)}, u32[]{:S(2)}, u32[]{:S(2)}) collective-permute-start(bf16[14,4,64,256]{3,2,1,0:T(8,128)(2,1)} %get-tuple-element.2858), channel_id=1, source_target_pairs={{0,16},{16,0},{1,17},{17,1},{2,18},{18,2},{3,19},{19,3},{4,20},{20... | collective-permute-start | bytes 5505032 | tf_op jit(solution)/shard_map/ppermute | solution.py:275
  199.4 165.4 %all-gather.15.cloned.1.call-start = ((), (), s32[]{:S(2)}) async-start(), calls=%async_computation.4 | async-start | bytes 2621440 | tf_op jit(solution)/shard_map/all_gather | solution.py:460
  247.4 45.3 %collective-permute-start.22 = (bf16[16,4,64,256]{3,2,1,0:T(8,128)(2,1)}, bf16[16,4,64,256]{3,2,1,0:T(8,128)(2,1)}, u32[]{:S(2)}, u32[]{:S(2)}) collective-permute-start(bf16[16,4,64,256]{3,2,1,0:T(8,128)(2,1)} %pad_maximum_fusion.14), channel_id=1, source_target_pairs={{0,16},{16,0},{1,17},{17,1},{2,18},{18,2},{3,19},{19,3},{4,20},{20... | collective-permute-start | bytes 6291464 | tf_op jit(solution)/shard_map/ppermute | solution.py:275
  256.4 67.4 %collective-permute-start.21 = (bf16[16,4,64,256]{3,2,1,0:T(8,128)(2,1)}, bf16[16,4,64,256]{3,2,1,0:T(8,128)(2,1)S(1)}, u32[]{:S(2)}, u32[]{:S(2)}) collective-permute-start(bf16[16,4,64,256]{3,2,1,0:T(8,128)(2,1)} %pad_maximum_fusion.13), channel_id=1, source_target_pairs={{0,8},{4,12},{8,0},{12,4},{1,9},{5,13},{9,1},{13,5},{2,10},{6,14},... | collective-permute-start | bytes 6291464 | tf_op jit(solution)/shard_map/ppermute | solution.py:275
  260.0 63.8 %collective-permute-start.18 = (bf16[1024,512]{1,0:T(8,128)(2,1)}, bf16[1024,512]{1,0:T(8,128)(2,1)S(1)}, u32[]{:S(2)}, u32[]{:S(2)}) collective-permute-start(bf16[1024,512]{1,0:T(8,128)(2,1)} %get-tuple-element.2900), channel_id=1, source_target_pairs={{0,8},{4,12},{9,1},{13,5},{18,26},{22,30},{27,19},{31,23},{8,24},{... | collective-permute-start | bytes 3145736 | tf_op jit(solution)/shard_map/ppermute | solution.py:478
  262.3 61.5 %collective-permute-start.17 = (bf16[1024,512]{1,0:T(8,128)(2,1)}, bf16[1024,512]{1,0:T(8,128)(2,1)}, u32[]{:S(2)}, u32[]{:S(2)}) collective-permute-start(bf16[1024,512]{1,0:T(8,128)(2,1)} %get-tuple-element.2901), channel_id=1, source_target_pairs={{0,16},{4,20},{9,25},{13,29},{18,2},{22,6},{27,11},{31,15},{16,24}... | collective-permute-start | bytes 3145736 | tf_op jit(solution)/shard_map/ppermute | solution.py:478
  267.8 137.4 %all-gather.9.cloned.1.call-start = ((), (), s32[]{:S(2)}) async-start(), calls=%async_computation.1 | async-start | bytes 2621440 | tf_op jit(solution)/shard_map/all_gather | solution.py:460
  327.7 37.1 %collective-permute-start.26 = (bf16[24,4,64,256]{3,2,1,0:T(8,128)(2,1)}, bf16[24,4,64,256]{3,2,1,0:T(8,128)(2,1)S(1)}, u32[]{:S(2)}, u32[]{:S(2)}) collective-permute-start(bf16[24,4,64,256]{3,2,1,0:T(8,128)(2,1)} %pad_maximum_fusion.9), channel_id=1, source_target_pairs={{0,4},{4,0},{8,12},{12,8},{1,5},{5,1},{9,13},{13,9},{2,6},{6,2},{1... | collective-permute-start | bytes 9437192 | tf_op jit(solution)/shard_map/ppermute | solution.py:275
  332.9 31.9 %collective-permute-start.25 = (bf16[24,4,64,256]{3,2,1,0:T(8,128)(2,1)}, bf16[24,4,64,256]{3,2,1,0:T(8,128)(2,1)}, u32[]{:S(2)}, u32[]{:S(2)}) collective-permute-start(bf16[24,4,64,256]{3,2,1,0:T(8,128)(2,1)} %pad_maximum_fusion.8), channel_id=1, source_target_pairs={{0,4},{4,0},{8,12},{12,8},{1,5},{5,1},{9,13},{13,9},{2,6},{6,2},{1... | collective-permute-start | bytes 9437192 | tf_op jit(solution)/shard_map/ppermute | solution.py:275
  340.0 100.6 %all-gather.11.cloned.1.call-start = ((), (), s32[]{:S(2)}) async-start(), calls=%async_computation.2 | async-start | bytes 2621440 | tf_op jit(solution)/shard_map/all_gather | solution.py:460
  372.1 33.1 %collective-permute-start.28 = (bf16[1024,512]{1,0:T(8,128)(2,1)}, bf16[1024,512]{1,0:T(8,128)(2,1)}, u32[]{:S(2)}, u32[]{:S(2)}) collective-permute-start(bf16[1024,512]{1,0:T(8,128)(2,1)} %get-tuple-element.2880), channel_id=1, source_target_pairs={{0,8},{4,12},{9,1},{13,5},{18,26},{22,30},{27,19},{31,23},{8,24},{... | collective-permute-start | bytes 3145736 | tf_op jit(solution)/shard_map/ppermute | solution.py:478
  374.5 30.7 %collective-permute-start.27 = (bf16[1024,512]{1,0:T(8,128)(2,1)}, bf16[1024,512]{1,0:T(8,128)(2,1)}, u32[]{:S(2)}, u32[]{:S(2)}) collective-permute-start(bf16[1024,512]{1,0:T(8,128)(2,1)} %get-tuple-element.2881), channel_id=1, source_target_pairs={{0,16},{4,20},{9,25},{13,29},{18,2},{22,6},{27,11},{31,15},{16,24}... | collective-permute-start | bytes 3145736 | tf_op jit(solution)/shard_map/ppermute | solution.py:478
  408.9 31.7 %collective-permute-start.32 = (bf16[2048,512]{1,0:T(8,128)(2,1)S(1)}, bf16[2048,512]{1,0:T(8,128)(2,1)}, u32[]{:S(2)}, u32[]{:S(2)}) collective-permute-start(bf16[2048,512]{1,0:T(8,128)(2,1)S(1)} %pad_maximum_fusion.18.refs_1_), channel_id=1, source_target_pairs={{0,4},{4,0},{8,12},{12,8},{1,5},{5,1},{9,13},{13,9},{2,6},{6,2},{1... | collective-permute-start | bytes 6291464 | tf_op jit(solution)/shard_map/ppermute | solution.py:275
  409.3 28.1 %collective-permute-start.31 = (bf16[1024,512]{1,0:T(8,128)(2,1)}, bf16[1024,512]{1,0:T(8,128)(2,1)S(1)}, u32[]{:S(2)}, u32[]{:S(2)}) collective-permute-start(bf16[1024,512]{1,0:T(8,128)(2,1)} %get-tuple-element.2874), channel_id=1, source_target_pairs={{0,8},{4,12},{9,1},{13,5},{18,26},{22,30},{27,19},{31,23},{8,24},{... | collective-permute-start | bytes 3145736 | tf_op jit(solution)/shard_map/ppermute | solution.py:478
  413.9 26.7 %collective-permute-start.30 = (bf16[1024,512]{1,0:T(8,128)(2,1)}, bf16[1024,512]{1,0:T(8,128)(2,1)}, u32[]{:S(2)}, u32[]{:S(2)}) collective-permute-start(bf16[1024,512]{1,0:T(8,128)(2,1)} %get-tuple-element.2875), channel_id=1, source_target_pairs={{0,16},{4,20},{9,25},{13,29},{18,2},{22,6},{27,11},{31,15},{16,24}... | collective-permute-start | bytes 3145736 | tf_op jit(solution)/shard_map/ppermute | solution.py:478
  444.4 41.2 %collective-permute-start.35 = (bf16[2048,512]{1,0:T(8,128)(2,1)S(1)}, bf16[2048,512]{1,0:T(8,128)(2,1)}, u32[]{:S(2)}, u32[]{:S(2)}) collective-permute-start(bf16[2048,512]{1,0:T(8,128)(2,1)S(1)} %pad_maximum_fusion.19.refs_2_), channel_id=1, source_target_pairs={{0,4},{4,0},{8,12},{12,8},{1,5},{5,1},{9,13},{13,9},{2,6},{6,2},{1... | collective-permute-start | bytes 6291464 | tf_op jit(solution)/shard_map/ppermute | solution.py:275
  445.6 40.0 %collective-permute-start.33 = (bf16[1024,512]{1,0:T(8,128)(2,1)}, bf16[1024,512]{1,0:T(8,128)(2,1)}, u32[]{:S(2)}, u32[]{:S(2)}) collective-permute-start(bf16[1024,512]{1,0:T(8,128)(2,1)} %get-tuple-element.2865), channel_id=1, source_target_pairs={{0,16},{4,20},{9,25},{13,29},{18,2},{22,6},{27,11},{31,15},{16,24}... | collective-permute-start | bytes 3145736 | tf_op jit(solution)/shard_map/ppermute | solution.py:478
  446.9 38.7 %collective-permute-start.34 = (bf16[1024,512]{1,0:T(8,128)(2,1)}, bf16[1024,512]{1,0:T(8,128)(2,1)}, u32[]{:S(2)}, u32[]{:S(2)}) collective-permute-start(bf16[1024,512]{1,0:T(8,128)(2,1)} %get-tuple-element.2866), channel_id=1, source_target_pairs={{0,8},{4,12},{9,1},{13,5},{18,26},{22,30},{27,19},{31,23},{8,24},{... | collective-permute-start | bytes 3145736 | tf_op jit(solution)/shard_map/ppermute | solution.py:478
  454.9 78.5 %collective-permute-start.40 = (bf16[1024,512]{1,0:T(8,128)(2,1)}, bf16[1024,512]{1,0:T(8,128)(2,1)}, u32[]{:S(2)}, u32[]{:S(2)}) collective-permute-start(bf16[1024,512]{1,0:T(8,128)(2,1)} %get-tuple-element.2864), channel_id=1, source_target_pairs={{0,16},{4,20},{9,25},{13,29},{18,2},{22,6},{27,11},{31,15}} | collective-permute-start | bytes 3145736 | tf_op jit(solution)/shard_map/ppermute | solution.py:478
  489.9 43.5 %collective-permute-start.39 = (bf16[1024,512]{1,0:T(8,128)(2,1)}, bf16[1024,512]{1,0:T(8,128)(2,1)S(1)}, u32[]{:S(2)}, u32[]{:S(2)}) collective-permute-start(bf16[1024,512]{1,0:T(8,128)(2,1)} %get-tuple-element.2867), channel_id=1, source_target_pairs={{0,8},{4,12},{9,1},{13,5},{18,26},{22,30},{27,19},{31,23}} | collective-permute-start | bytes 3145736 | tf_op jit(solution)/shard_map/ppermute | solution.py:478
  491.2 42.2 %collective-permute-start.37 = (bf16[1024,512]{1,0:T(8,128)(2,1)}, bf16[1024,512]{1,0:T(8,128)(2,1)S(1)}, u32[]{:S(2)}, u32[]{:S(2)}) collective-permute-start(bf16[1024,512]{1,0:T(8,128)(2,1)} %collective-permute-done.33), channel_id=1, source_target_pairs={{16,24},{20,28},{25,17},{29,21},{2,10},{6,14},{11,3},{15,7},{24,8}... | collective-permute-start | bytes 3145736 | tf_op jit(solution)/shard_map/ppermute | solution.py:478
  492.5 40.9 %collective-permute-start.38 = (bf16[1024,512]{1,0:T(8,128)(2,1)}, bf16[1024,512]{1,0:T(8,128)(2,1)}, u32[]{:S(2)}, u32[]{:S(2)}) collective-permute-start(bf16[1024,512]{1,0:T(8,128)(2,1)} %collective-permute-done.34), channel_id=1, source_target_pairs={{8,24},{12,28},{1,17},{5,21},{26,10},{30,14},{19,3},{23,7},{24,16}... | collective-permute-start | bytes 3145736 | tf_op jit(solution)/shard_map/ppermute | solution.py:478
  (43 other events, 778.8 us)
Sparse Core Ops, SparseCore 0:
  13.3 47.1 all-gather.6
  182.4 46.4 all-gather.16
  230.4 44.6 all-gather.12
  276.6 44.6 all-gather.14
  340.1 47.4 all-gather.8
  389.0 44.5 all-gather.10

commit v2 on v1

--- a/solution.py
+++ b/solution.py
@@ -9,7 +9,8 @@
 from jax.sharding import PartitionSpec as P
 
 COL_WINDOW = 8
-ROW_WINDOWS = (14, 8, 6)
+ROW_WINDOWS = (15, 9, 6)
+MORE_COLUMNS = 2
 CHUNKS = 6
 VMEM = 56 * 1024 * 1024
 
@@ -142,19 +143,15 @@
     )(panel, inverses)
 
 
-def extend_kernel(tile, parts, groups, order, count, row_at, col_at, me, base_ref, *refs):
+def extend_kernel(tile, parts, groups, row_at, col_at, me, base_ref, *refs):
     strips, out_ref = refs[:-1], refs[-1]
-    i = pl.program_id(0)
+    p = pl.program_id(0)
     part = tile // parts
     window = col_at.shape[1] // groups
-
-    @pl.when((i == 0) | (i < count[0]))
-    def _():
-        out_ref[...] = base_ref[...]
-
+    out_ref[...] = base_ref[...]
     for kid, group in itertools.product(range(2), range(groups)):
 
-        @pl.when((i < count[0]) & (row_at[kid * parts, order[i]] >= 0))
+        @pl.when(row_at[kid * parts, p] >= 0)
         def _():
             @pl.loop(0, window)
             def _(b):
@@ -170,39 +167,34 @@
                         out_ref[here] += strip_ref[0, b].astype(jnp.float32)
 
 
-def extend_add(base, strips, tables, me, tile):
+def extend_add(base, strips, tables, me, tile, in_place):
     height, width = base.shape
     parts = tile // strips[0].shape[2]
     groups = len(strips) // (2 * parts)
-    order, count, row_at, col_at = tables
+    row_at, col_at = tables
 
     def strip_spec(i):
         return pl.BlockSpec(
             (1,) + strips[i].shape[1:],
-            lambda p, order, count, row_at, *_: (
-                jnp.maximum(row_at[i % (2 * parts), order[p]], 0),
-                0,
-                0,
-                0,
-            ),
+            lambda p, row_at, *_: (jnp.maximum(row_at[i % (2 * parts), p], 0), 0, 0, 0),
         )
 
-    block = pl.BlockSpec((tile, width), lambda p, order, *_: (order[p], 0))
+    block = pl.BlockSpec((tile, width), lambda p, *_: (p, 0))
     return pl.pallas_call(
         functools.partial(extend_kernel, tile, parts, groups),
         grid_spec=pltpu.PrefetchScalarGridSpec(
-            num_scalar_prefetch=5,
+            num_scalar_prefetch=3,
             grid=(height // tile,),
             in_specs=[block] + [strip_spec(i) for i in range(len(strips))],
             out_specs=block,
         ),
         out_shape=jax.ShapeDtypeStruct(base.shape, base.dtype),
-        input_output_aliases={5: 0},
+        input_output_aliases={3: 0} if in_place else {},
         compiler_params=pltpu.CompilerParams(vmem_limit_bytes=VMEM),
         cost_estimate=pl.CostEstimate(
-            flops=base.size, bytes_accessed=4 * base.size, transcendentals=0
+            flops=base.size, bytes_accessed=8 * base.size, transcendentals=0
         ),
-    )(order, count.reshape(1), row_at, col_at, me.reshape(1), base, *strips)
+    )(row_at, col_at, me.reshape(1), base, *strips)
 
 
 def update_kernel(tile, count, core, mask, *refs):
@@ -238,17 +230,21 @@
     return (c // per_side ^ core[0]) * per_side + c % per_side
 
 
-def update(base, rows, mine, other, mask, core, tile, in_place):
+def update(base, rows, mine, other, mask, core, tile):
     height, width = base.shape
-    step = 4 * tile
+    step = 2 * tile
     per_side = width // step // 2
-    block = pl.BlockSpec((step, step), lambda i, c, core, _: (i, column_block(c, per_side, core)))
+    block = pl.BlockSpec((height, step), lambda i, c, core, _: (i, column_block(c, per_side, core)))
     row_block = lambda i, c, *_: (i, 0)
     mine_block = lambda i, c, *_: (jnp.minimum(c, per_side - 1), 0)
     other_block = lambda i, c, *_: (jnp.maximum(c - per_side, 0), 0)
     specs = [
-        pl.BlockSpec((step, piece.shape[1]), at)
-        for pieces, at in ((rows, row_block), (mine, mine_block), (other, other_block))
+        pl.BlockSpec((size, piece.shape[1]), at)
+        for pieces, size, at in (
+            (rows, height, row_block),
+            (mine, step, mine_block),
+            (other, step, other_block),
+        )
         for piece in pieces
     ]
     depth = sum(piece.shape[1] for piece in rows)
@@ -256,12 +252,12 @@
         functools.partial(update_kernel, tile, len(rows)),
         grid_spec=pltpu.PrefetchScalarGridSpec(
             num_scalar_prefetch=2,
-            grid=(height // step, width // step),
+            grid=(1, width // step),
             in_specs=specs + [block],
             out_specs=block,
         ),
         out_shape=jax.ShapeDtypeStruct(base.shape, base.dtype),
-        input_output_aliases={2 + 3 * len(rows): 0} if in_place else {},
+        input_output_aliases={2 + 3 * len(rows): 0},
         compiler_params=pltpu.CompilerParams(vmem_limit_bytes=VMEM),
         cost_estimate=pl.CostEstimate(
             flops=2 * height * width * depth, bytes_accessed=8 * base.size, transcendentals=0
@@ -294,9 +290,6 @@
     own_rows, own_cols = child.shape[0] // tile, child.shape[1] // tile
     child_tiles = child_map.shape[1]
     part = tile // rows
-    col_window = min(COL_WINDOW, child_tiles)
-    row_windows = [min(size, child_tiles) for size in ROW_WINDOWS]
-
     def send_strips():
         shaped = child.reshape(own_rows, rows, part, own_cols, tile).transpose(1, 0, 3, 2, 4)
         return [
@@ -315,143 +308,143 @@
 
     col_edges = edges_of(planes)
     row_edges = [edges_of(count) for count in (subs, subs * rows // cores, grid)]
-    rounds = [rounds_of(col_edges, col_window)]
-    rounds += [rounds_of(edges, size) for edges, size in zip(row_edges, row_windows)]
-
-    def turns_of(turn):
+    def turns_of(turn, rounds):
         turns = []
         for count in reversed(rounds):
             turns.append(turn % count)
             turn = turn // count
         return turns[::-1]
 
-    def col_start(kid, plane, turn):
-        return jnp.minimum(col_edges[kid, plane] + turn * col_window, child_tiles - col_window)
-
-    def row_starts(kid, row, turns):
-        start, size, found = 0, child_tiles, []
-        places_at = (row // rows, row // cores, row)
-        for edges, at, turn, window in zip(row_edges, places_at, turns, row_windows):
-            start = jnp.clip(edges[kid, at] + turn * window, start, start + size - window)
-            size = window
-            found.append(start)
-        return found
-
-    def send_columns(strips, turn):
-        stripped = jnp.zeros((own_rows, child_tiles, part, tile), child.dtype)
-        for m, got in enumerate(strips):
-            stripped = lax.dynamic_update_slice(stripped, got, (0, (r ^ m) * own_cols, 0, 0))
-        pieces = []
-        for m in range(planes):
-            start = col_start(s, z ^ m, turn)
-            piece = lax.dynamic_slice_in_dim(stripped, start, col_window, 1)
-            pieces.append(xor_permute(piece, "col", planes, m))
-        return pieces
-
-    def join_columns(pieces):
-        groups = []
-        for half in range(2):
-            placed = jnp.zeros((child_tiles, col_window // 2, part, tile), child.dtype)
-            for m, got in enumerate(pieces):
-                got = got[:, half * col_window // 2 : (half + 1) * col_window // 2]
-                placed = lax.dynamic_update_slice(placed, got, ((z ^ m) * own_rows, 0, 0, 0))
-            groups.append(placed)
-        return groups
-
-    def taken(value, start, size):
-        return lax.dynamic_slice_in_dim(value, start, size, 0)
-
     kids = (s, 1 - s)
 
-    size = row_windows[1]
-
-    def rows_for(values, row, turns, level=None):
-        parts = []
-        for value, kid in zip(values, kids):
-            found = row_starts(kid, row, turns)
-            first = 0 if level is None else found[level]
-            parts.append(taken(value, found[1] - first, size))
-        return parts
-
-    def halves_first(placed, turns):
-        here, there = (row_starts(s, row, turns)[0] for row in (grid_row, grid_row ^ rows))
-        window = row_windows[0]
-        return [
-            taken(placed, here, window),
-            xor_permute(taken(placed, there, window), "sub", subs, 1),
-        ]
-
-    def chips_second(halves, turns):
-        here, there = (
-            jnp.concatenate(rows_for(halves, row, turns, 0), axis=0)
-            for row in (grid_row, grid_row ^ cores)
-        )
-        return [here, xor_permute(there, "row", rows, cores)]
-
-    def chips_first(placed, turns):
-        def of_both_halves(row):
-            found = [rows_for([placed], half * rows + row, turns)[0] for half in range(subs)]
-            return jnp.concatenate(found, axis=0)
-
-        return [of_both_halves(r), xor_permute(of_both_halves(r ^ cores), "row", rows, cores)]
-
-    def halves_second(strips, turns):
-        here, there = (
-            [taken(strip, half * size, size) for strip in strips] for half in kids
-        )
-        got = xor_permute(jnp.concatenate(there, axis=0), "sub", subs, 1)
-        return [
-            jnp.concatenate((kept, got[k * size : (k + 1) * size]), axis=0)
-            for k, kept in enumerate(here)
-        ]
-
-    def send_cores(strips, turns):
-        found = [row_starts(kid, grid_row ^ 1, turns) for kid in kids]
-        parts = [
-            taken(strip, kid * size + at[2] - at[1], row_windows[2])
-            for strip in strips
-            for kid, at in enumerate(found)
-        ]
-        return xor_permute(jnp.concatenate(parts, axis=0), "row", rows, 1)
-
-    def tables_of(turns):
-        col_turn, row_turns = turns[0], turns[1:]
-        col_at, row_at = [], []
-        wanted = grid_row * tile_rows + jnp.arange(tile_rows, dtype=jnp.int32)
-        for place, kid in enumerate(kids):
-            own_map = lax.dynamic_index_in_dim(child_map, kid, 0, keepdims=False)
-            first = col_edges[kid, z] + col_turn * col_window
-            last = jnp.minimum(first + col_window, col_edges[kid, z + 1])
-            start = col_start(kid, z, col_turn)
-            slot = start + jnp.arange(col_window, dtype=jnp.int32)
-            parent = lax.dynamic_slice_in_dim(own_map, start, col_window) - z * tile_cols
-            col_at.append(jnp.where((slot >= first) & (slot < last), parent, -1))
-
-            same = own_map[None, :] == wanted[:, None]
-            slot = jnp.max(jnp.where(same, jnp.arange(child_tiles, dtype=jnp.int32), -1), axis=1)
-            held = slot >= 0
-            at_level = (s, chip, grid_row)
-            for edges, at, turn, window in zip(row_edges, at_level, row_turns, row_windows):
-                first = edges[kid, at] + turn * window
-                held &= (slot >= first) & (slot < first + window)
-            starts = row_starts(kid, grid_row, row_turns)
-            near_at = place * row_windows[1] + slot - starts[1]
-            far_at = [(k * 2 + place) * row_windows[2] + slot - starts[2] for k in range(2)]
-            order = (near_at, far_at[0], near_at, far_at[1])
-            row_at += [jnp.where(held, at, -1) for at in order]
-        row_at, col_at = jnp.stack(row_at), jnp.stack(col_at)
-        reached = jnp.max(row_at, axis=0) >= 0
-        count = jnp.sum(reached, dtype=jnp.int32)
-        every = jnp.arange(tile_rows, dtype=jnp.int32)
-        before = jnp.sum(reached[None, :] & (every[None, :] < every[:, None]), axis=1, dtype=jnp.int32)
-        wanted = jnp.minimum(every, jnp.maximum(count - 1, 0))
-        listed = reached[None, :] & (before[None, :] == wanted[:, None])
-        order = jnp.max(jnp.where(listed, every[None, :], 0), axis=1)
-        return order, count, row_at, col_at
-
-    def extend(base, near, far, tables):
+    def router(col_base, col_window, row_windows):
+        def col_start(kid, plane, turn):
+            return jnp.minimum(col_edges[kid, plane] + col_base + turn * col_window, child_tiles - col_window)
+
+        def row_starts(kid, row, turns):
+            start, size, found = 0, child_tiles, []
+            places_at = (row // rows, row // cores, row)
+            for edges, at, turn, window in zip(row_edges, places_at, turns, row_windows):
+                start = jnp.clip(edges[kid, at] + turn * window, start, start + size - window)
+                size = window
+                found.append(start)
+            return found
+
+        def send_columns(strips, turn):
+            stripped = jnp.zeros((own_rows, child_tiles, part, tile), child.dtype)
+            for m, got in enumerate(strips):
+                stripped = lax.dynamic_update_slice(stripped, got, (0, (r ^ m) * own_cols, 0, 0))
+            pieces = []
+            for m in range(planes):
+                start = col_start(s, z ^ m, turn)
+                piece = lax.dynamic_slice_in_dim(stripped, start, col_window, 1)
+                pieces.append(xor_permute(piece, "col", planes, m))
+            return pieces
+
+        def join_columns(pieces):
+            groups = []
+            for half in range(2):
+                placed = jnp.zeros((child_tiles, col_window // 2, part, tile), child.dtype)
+                for m, got in enumerate(pieces):
+                    got = got[:, half * col_window // 2 : (half + 1) * col_window // 2]
+                    placed = lax.dynamic_update_slice(placed, got, ((z ^ m) * own_rows, 0, 0, 0))
+                groups.append(placed)
+            return groups
+
+        def taken(value, start, size):
+            return lax.dynamic_slice_in_dim(value, start, size, 0)
+
+        size = row_windows[1]
+
+        def rows_for(values, row, turns, level=None):
+            parts = []
+            for value, kid in zip(values, kids):
+                found = row_starts(kid, row, turns)
+                first = 0 if level is None else found[level]
+                parts.append(taken(value, found[1] - first, size))
+            return parts
+
+        def halves_first(placed, turns):
+            here, there = (row_starts(s, row, turns)[0] for row in (grid_row, grid_row ^ rows))
+            window = row_windows[0]
+            return [
+                taken(placed, here, window),
+                xor_permute(taken(placed, there, window), "sub", subs, 1),
+            ]
+
+        def chips_second(halves, turns):
+            here, there = (
+                jnp.concatenate(rows_for(halves, row, turns, 0), axis=0)
+                for row in (grid_row, grid_row ^ cores)
+            )
+            return [here, xor_permute(there, "row", rows, cores)]
+
+        def chips_first(placed, turns):
+            def of_both_halves(row):
+                found = [rows_for([placed], half * rows + row, turns)[0] for half in range(subs)]
+                return jnp.concatenate(found, axis=0)
+
+            return [of_both_halves(r), xor_permute(of_both_halves(r ^ cores), "row", rows, cores)]
+
+        def halves_second(strips, turns):
+            here, there = (
+                [taken(strip, half * size, size) for strip in strips] for half in kids
+            )
+            got = xor_permute(jnp.concatenate(there, axis=0), "sub", subs, 1)
+            return [
+                jnp.concatenate((kept, got[k * size : (k + 1) * size]), axis=0)
+                for k, kept in enumerate(here)
+            ]
+
+        def send_cores(strips, turns):
+            found = [row_starts(kid, grid_row ^ 1, turns) for kid in kids]
+            parts = [
+                taken(strip, kid * size + at[2] - at[1], row_windows[2])
+                for strip in strips
+                for kid, at in enumerate(found)
+            ]
+            return xor_permute(jnp.concatenate(parts, axis=0), "row", rows, 1)
+
+        def tables_of(turns):
+            col_turn, row_turns = turns[0], turns[1:]
+            col_at, row_at = [], []
+            wanted = grid_row * tile_rows + jnp.arange(tile_rows, dtype=jnp.int32)
+            for place, kid in enumerate(kids):
+                own_map = lax.dynamic_index_in_dim(child_map, kid, 0, keepdims=False)
+                first = col_edges[kid, z] + col_base + col_turn * col_window
+                last = jnp.minimum(first + col_window, col_edges[kid, z + 1])
+                start = col_start(kid, z, col_turn)
+                slot = start + jnp.arange(col_window, dtype=jnp.int32)
+                parent = lax.dynamic_slice_in_dim(own_map, start, col_window) - z * tile_cols
+                col_at.append(jnp.where((slot >= first) & (slot < last), parent, -1))
+
+                same = own_map[None, :] == wanted[:, None]
+                slot = jnp.max(jnp.where(same, jnp.arange(child_tiles, dtype=jnp.int32), -1), axis=1)
+                held = slot >= 0
+                at_level = (s, chip, grid_row)
+                for edges, at, turn, window in zip(row_edges, at_level, row_turns, row_windows):
+                    first = edges[kid, at] + turn * window
+                    held &= (slot >= first) & (slot < first + window)
+                starts = row_starts(kid, grid_row, row_turns)
+                near_at = place * row_windows[1] + slot - starts[1]
+                far_at = [(k * 2 + place) * row_windows[2] + slot - starts[2] for k in range(2)]
+                order = (near_at, far_at[0], near_at, far_at[1])
+                row_at += [jnp.where(held, at, -1) for at in order]
+            return jnp.stack(row_at), jnp.stack(col_at)
+
+        def first_rows(placed, turns):
+            return halves_first(placed[0], turns), chips_first(placed[1], turns)
+
+        def second_rows(first, turns):
+            return chips_second(first[0], turns), halves_second(first[1], turns)
+
+        def third_rows(near, turns):
+            return [send_cores(group, turns) for group in near]
+        return send_columns, join_columns, first_rows, second_rows, third_rows, tables_of
+
+    def extend(base, near, far, tables, in_place=True):
         strips = [strip for (a, b), c in zip(near, far) for strip in (a, c, b, c) * 2]
-        return extend_add(base, strips, tables, r, tile)
+        return extend_add(base, strips, tables, r, tile, in_place)
 
     fence = lax.optimization_barrier
     chunks, child = fence((chunks, child))
@@ -508,70 +501,76 @@
         pattern, (grid_row * tile_rows, z * tile_cols), (tile_rows, tile_cols)
     )
 
-    def subtract(base, first, columns, in_place=True):
+    def subtract(base, first, columns):
         mine, other = zip(*columns)
         part = row_chunks[first : first + len(columns)]
-        return update(base, part, mine, other, local_mask, core, tile, in_place)
+        return update(base, part, mine, other, local_mask, core, tile)
 
     no_turns = [0] * 4
     row_turns = no_turns[1:]
     strips = fence(send_strips())
 
+    col_window = min(COL_WINDOW, child_tiles)
+    row_windows = [min(size, child_tiles) for size in ROW_WINDOWS]
+    send_columns, join_columns, first_rows, second_rows, third_rows, tables_of = router(
+        0, col_window, row_windows
+    )
     got = beat(0, [])
     pieces = send_columns(strips, 0)
     tables = tables_of(no_turns)
     got, pieces, chunks, tables, local_mask = fence((got, pieces, chunks, tables, local_mask))
     row_chunks = row_chunks + gather(chunks[1:])
 
-    def first_rows(placed, turns):
-        return halves_first(placed[0], turns), chips_first(placed[1], turns)
-
-    def second_rows(first, turns):
-        return chips_second(first[0], turns), halves_second(first[1], turns)
-
-    def third_rows(near, turns):
-        return [send_cores(group, turns) for group in near]
-
-    halfway = fence(first_rows(join_columns(pieces), row_turns))
+    placed = join_columns(pieces)
+    halfway = first_rows(placed, row_turns)
+    got = beat(1, got)
+    got, halfway = fence((got, halfway))
 
     near = second_rows(halfway, row_turns)
-    got = beat(1, got)
-    got, near = fence((got, near))
-
+    got, near, row_chunks[2] = fence((got, near, row_chunks[2]))
+
+    got = beat(2, got)
     far = third_rows(near, row_turns)
-    got = beat(2, got)
-    got, far = fence((got, far))
-
-    columns = [columns_of(0, got)]
-    base = subtract(front_trailing, 0, columns, False)
-    got = beat(3, got)
-    got, base = fence((got, base))
-
-    columns.append(columns_of(1, got))
-    base = extend(base, near, far, tables)
-    got = beat(4, got)
-    got, base, columns = fence((got, base, columns))
-
-    columns.append(columns_of(2, got))
-    base = subtract(base, 1, columns[1:2])
+    base = extend(front_trailing, near, far, tables, False)
+    got = beat(4, beat(3, got))
+    columns = [columns_of(c, got) for c in (0, 1)]
+    got, base, columns, row_chunks[5] = fence((got, base, columns, row_chunks[5]))
+
+    row_rounds = [rounds_of(edges, size) for edges, size in zip(row_edges, row_windows)]
+    every_round = functools.reduce(lambda a, b: a * b, row_rounds)
+
+    def more_rows(turn, base):
+        turns = turns_of(turn, row_rounds)
+        near = second_rows(first_rows(placed, turns), turns)
+        return extend(base, near, third_rows(near, turns), tables_of([0] + turns))
+
+    base = lax.fori_loop(1, every_round, more_rows, base)
+
+    most = jnp.max(col_edges[:, 1:] - col_edges[:, :-1])
+    ranges = [pattern.shape[0] // count for count in (subs, subs * rows // cores, grid)]
+    sends, joins, firsts, seconds, thirds, tables_at = router(
+        col_window, MORE_COLUMNS, [min(size, child_tiles) for size in ranges]
+    )
+
+    def more_columns(turn, base):
+        near = seconds(firsts(joins(sends(strips, turn)), row_turns), row_turns)
+        return extend(base, near, thirds(near, row_turns), tables_at([turn] + row_turns))
+
+    left = jnp.maximum(most - col_window, 0)
+    base = lax.fori_loop(0, (left + MORE_COLUMNS - 1) // MORE_COLUMNS, more_columns, base)
+
+    base = subtract(base, 0, columns)
+    columns = [columns_of(2, got)]
     got = beat(5, got)
     got, base, columns = fence((got, base, columns))
 
-    columns.append(columns_of(3, got))
+    base = subtract(base, 2, columns)
     straight = [hand_on(held, [(0, way[3])]) for held, way in zip(halves_of(5), ring)]
     got = beat(6, got)
 
-    def more(turn, base):
-        turns = turns_of(turn)
-        placed = join_columns(send_columns(strips, turns[0]))
-        near = second_rows(first_rows(placed, turns[1:]), turns[1:])
-        return extend(base, near, third_rows(near, turns[1:]), tables_of(turns))
-
-    every_round = functools.reduce(lambda a, b: a * b, rounds)
-    base = lax.fori_loop(1, every_round, more, base)
-    base = subtract(base, 2, columns[2:])
     base, got, straight = fence((base, got, straight))
-    base = subtract(base, 4, [columns_of(4, got), columns_of(5, got, straight)])
+    columns = [columns_of(3, got), columns_of(4, got), columns_of(5, got, straight)]
+    base = subtract(base, 3, columns)
     return (factor, base)
 
 

time: 596 us -> 628 us (1.054)
  Pallas kernels: 157 us -> 134 us
  waiting for transfers between devices: 240 us -> 257 us
  between operations: 43.4 us -> 57.6 us
  local copies, waits for them, and re-layouts: 46.3 us -> 57.5 us
    pallas_call x4 -> x3, Pallas kernels: 129 us -> 101 us  [update(): pl.pallas_call(functools.partial(update_kernel, tile, len(rows)), grid_sp...]
    all_gather x6, waiting for transfers between devices: 0.04 us -> 16.1 us  [gather(): lax.all_gather(piece, 'col', axis=0, tiled=True)]
  transfers between devices with their start and end apart: 40 -> 40, of which waited for: 14 -> 16; matrix products, arithmetic and copies ran while one was open for 14% -> 16% of each run, Pallas kernels for 20% -> 15%
where the time goes in v2:
time: 628 us; the launch traced here: 617 us
  waiting for transfers between devices  257 us (41%)
  Pallas kernels  134 us (21%)
  between operations  57.6 us (9%)
  local copies, waits for them, and re-layouts  57.5 us (9%)
  starting transfers between devices  56.1 us (9%)
  other arithmetic  53.6 us (9%)
    ppermute x18, waiting for transfers between devices, xor_permute(): return lax.ppermute(value, axes, [(i, i ^ mask) for i in range(size)])  189 us
    pallas_call x3, Pallas kernels, update(): pl.pallas_call(functools.partial(update_kernel, tile, len(rows)), grid_sp...  101 us
    ppermute x16, waiting for transfers between devices, hand_on(): return lax.ppermute(held, ('sub', 'row', 'col'), pairs)  51.1 us
    ppermute x16, starting transfers between devices, hand_on(): return lax.ppermute(held, ('sub', 'row', 'col'), pairs)  34.7 us
    pallas_call x1, Pallas kernels, extend_add(): pl.pallas_call(functools.partial(extend_kernel, tile, parts, groups), gri...  27.3 us
    ppermute x18, starting transfers between devices, xor_permute(): return lax.ppermute(value, axes, [(i, i ^ mask) for i in range(size)])  21.1 us
    select_n x4, other arithmetic, beat(): held = jnp.where(place == 0, held, got[at - 1][side])  17.6 us
    dynamic_slice x10, local copies, waits for them, and re-layouts, taken(): return lax.dynamic_slice_in_dim(value, start, size, 0)  16.3 us
  transfers between devices with their start and end apart: 40, of which 16 were waited for; matrix products, arithmetic and copies ran while one was open for 16% of the time, Pallas kernels for 15%

profile of v2, /device:TPU:5, one launch (start us, length us, event | category | flops | bytes accessed | tf_op | source)
XLA Modules:
  0.0 616.8 jit_solution(5151167917055027220)
XLA Ops:
  7.2 6.0 shard_map.77
  13.3 5.6 reshape.993
  18.9 3.9 constant_dynamic-slice_fusion.56
  34.1 11.8 %collective-permute-done.18 = bf16[5,5,64,256]{3,2,1,0:T(8,128)(2,1)S(1)} collective-permute-done((bf16[5,5,64,256]{3,2,1,0:T(8,128)(2,1)}, bf16[5,5,64,256]{3,2,1,0:T(8,128)(2,1)S(1)}, u32[]{:S(2)}, u32[]{:S(2)}) %collective-permute-start.18) | collective-permute-done | bytes 819232 | tf_op jit(solution)/shard_map/ppermute | solution.py:271
  45.9 17.5 %collective-permute-done.19 = bf16[5,5,64,256]{3,2,1,0:T(8,128)(2,1)S(1)} collective-permute-done((bf16[5,5,64,256]{3,2,1,0:T(8,128)(2,1)}, bf16[5,5,64,256]{3,2,1,0:T(8,128)(2,1)S(1)}, u32[]{:S(2)}, u32[]{:S(2)}) %collective-permute-start.19) | collective-permute-done | bytes 819232 | tf_op jit(solution)/shard_map/ppermute | solution.py:271
  88.9 3.7 select_bitcast_fusion.12
  99.0 83.2 %collective-permute-done.21 = bf16[5,8,64,256]{3,2,1,0:T(8,128)(2,1)} collective-permute-done((bf16[5,8,64,256]{3,2,1,0:T(8,128)(2,1)}, bf16[5,8,64,256]{3,2,1,0:T(8,128)(2,1)}, u32[]{:S(2)}, u32[]{:S(2)}) %collective-permute-start.21) | collective-permute-done | bytes 1310752 | tf_op jit(solution)/shard_map/ppermute | solution.py:271
  201.1 4.0 constant_dynamic-slice_fusion.45
  207.5 3.9 constant_dynamic-slice_fusion.48
  212.8 16.1 %all-gather.13.cloned.1.call-done.refs_1_ = bf16[2048,512]{1,0:T(8,128)(2,1)} async-done(((bf16[512,512]{1,0:T(8,128)(2,1)}), bf16[2048,512]{1,0:T(8,128)(2,1)}) %all-gather.13.cloned.1.call-update) | async-done | bytes 2097168 | tf_op jit(solution)/shard_map/all_gather | solution.py:453
  228.9 3.7 broadcast_select_fusion.8
  238.8 15.8 %collective-permute-done.25 = bf16[15,4,64,256]{3,2,1,0:T(8,128)(2,1)} collective-permute-done((bf16[15,4,64,256]{3,2,1,0:T(8,128)(2,1)}, bf16[15,4,64,256]{3,2,1,0:T(8,128)(2,1)}, u32[]{:S(2)}, u32[]{:S(2)}) %collective-permute-start.25) | collective-permute-done | bytes 1966112 | tf_op jit(solution)/shard_map/ppermute | solution.py:271
  254.6 4.0 collective-permute-done.26
  258.7 22.5 %collective-permute-done.24 = bf16[1024,512]{1,0:T(8,128)(2,1)} collective-permute-done((bf16[1024,512]{1,0:T(8,128)(2,1)}, bf16[1024,512]{1,0:T(8,128)(2,1)}, u32[]{:S(2)}, u32[]{:S(2)}) %collective-permute-start.24) | collective-permute-done | bytes 1048608 | tf_op jit(solution)/shard_map/ppermute | solution.py:471
  296.3 40.8 %collective-permute-done.28 = bf16[18,4,64,256]{3,2,1,0:T(8,128)(2,1)} collective-permute-done((bf16[18,4,64,256]{3,2,1,0:T(8,128)(2,1)}, bf16[18,4,64,256]{3,2,1,0:T(8,128)(2,1)}, u32[]{:S(2)}, u32[]{:S(2)}) %collective-permute-start.28) | collective-permute-done | bytes 2359328 | tf_op jit(solution)/shard_map/ppermute | solution.py:271
  341.0 4.3 collective-permute-done.27.refs_2_.refs_6_
  345.3 3.7 broadcast_select_fusion.6
  356.3 16.3 %collective-permute-done.30 = bf16[1024,512]{1,0:T(8,128)(2,1)S(1)} collective-permute-done((bf16[1024,512]{1,0:T(8,128)(2,1)}, bf16[1024,512]{1,0:T(8,128)(2,1)S(1)}, u32[]{:S(2)}, u32[]{:S(2)}) %collective-permute-start.30) | collective-permute-done | bytes 1048608 | tf_op jit(solution)/shard_map/ppermute | solution.py:471
  374.6 3.6 broadcast_select_fusion.4
  384.4 4.2 collective-permute-start.36
  393.1 7.8 %collective-permute-done.32 = bf16[1024,512]{1,0:T(8,128)(2,1)} collective-permute-done((bf16[1024,512]{1,0:T(8,128)(2,1)}, bf16[1024,512]{1,0:T(8,128)(2,1)}, u32[]{:S(2)}, u32[]{:S(2)}) %collective-permute-start.32) | collective-permute-done | bytes 1048608 | tf_op jit(solution)/shard_map/ppermute | solution.py:471
  403.3 6.6 %broadcast_select_fusion.2 = (bf16[1024,512]{1,0:T(8,128)(2,1)}, bf16[1024,512]{1,0:T(8,128)(2,1)}, bf16[1024,512]{1,0:T(8,128)(2,1)S(1)}, bf16[1024,512]{1,0:T(...) fusion(bf16[1024,512]{1,0:T(8,128)(2,1)} %collective-permute-done.32, pred[]{:T(512)S(6)} %eq.233, ...), kind=kLoop, calls=%fused_computation.155 | loop fusion | flops 7340032 | bytes 20971524 | tf_op jit(solution)/shard_map/jit(_where)/select_n | solution.py:483
  411.4 5.1 collective-permute-start.38
  440.2 27.3 %shard_map.78 = f32[2048,4096]{1,0:T(8,128)} custom-call(s32[8,8]{1,0:T(8,128)} %stack.40.row_at, s32[2,8]{1,0:T(2,128)} %pad_add_fusion.2.col_at, s32[1]{0:T(128)} %bitcast.93.me, f32[2048,4096]{1,0:T(8,128)} %base_ref.1, bf16[18,4,64,256]{3,2,1,0:T(8,128)(2,1)} %pad_maximum_fusion.20.refs_0_.refs_4_, ...), custom_call_target="tpu_custom_call" | custom-call | flops 8388608 | bytes 67108864 | tf_op jit(solution)/shard_map/pallas_call | solution.py:183
  467.5 4.9 fusion.25
  477.8 6.0 collective-permute-start.40
  485.1 34.6 %shard_map.79.refs_3_ = f32[2048,4096]{1,0:T(8,128)} custom-call(s32[1]{0:T(128)} %bitcast.51.core, s32[8,16]{1,0:T(8,128)} %dynamic_slice.1092.mask, bf16[2048,512]{1,0:T(8,128)(2,1)} %all-gather.7.cloned.1.call-done.refs_0_, bf16[2048,512]{1,0:T(8,128)(2,1)} %all-gather.13.cloned.1.call-done.refs_1_, ...), custom_call_target="tpu_custom_call", output_to_operand_aliasing={{}: (8, {})} | custom-call | flops 17179869184 | bytes 67108864 | tf_op jit(solution)/shard_map/pallas_call | solution.py:251
  521.3 5.7 collective-permute-start.43
  527.0 28.3 %shard_map.80.refs_9_ = f32[2048,4096]{1,0:T(8,128)} custom-call(s32[1]{0:T(128)} %bitcast.51.core, s32[8,16]{1,0:T(8,128)} %dynamic_slice.1092.mask, bf16[2048,512]{1,0:T(8,128)(2,1)} %all-gather.15.cloned.1.call-done.refs_0_, bf16[2048,512]{1,0:T(8,128)(2,1)} %pad_maximum_fusion.27.refs_1_, ...), custom_call_target="tpu_custom_call", output_to_operand_aliasing={{}: (5, {})} | custom-call | flops 8589934592 | bytes 67108864 | tf_op jit(solution)/shard_map/pallas_call | solution.py:251
  555.3 3.6 select_select_fusion.1
  563.8 6.0 collective-permute-done.47.refs_7_
  571.2 38.3 %shard_map.81 = f32[2048,4096]{1,0:T(8,128)} custom-call(s32[1]{0:T(128)} %bitcast.51.core, s32[8,16]{1,0:T(8,128)} %dynamic_slice.1092.mask, bf16[2048,512]{1,0:T(8,128)(2,1)} %all-gather.9.cloned.1.call-done.refs_0_, bf16[2048,512]{1,0:T(8,128)(2,1)} %all-gather.11.cloned.1.call-done.refs_1_, ...), custom_call_target="tpu_custom_call", output_to_operand_aliasing={{}: (11, {})} | custom-call | flops 25769803776 | bytes 67108864 | tf_op jit(solution)/shard_map/pallas_call | solution.py:251
  (193 shorter events, 110.5 us)
Async XLA Ops:
  7.2 63.0 %all-gather.7.cloned.1.call-start = ((), (), s32[]{:S(2)}) async-start(), calls=%async_computation | async-start | bytes 2621440 | tf_op jit(solution)/shard_map/all_gather | solution.py:453
  13.2 215.7 %all-gather.13.cloned.1.call-start = ((), (), s32[]{:S(2)}) async-start(), calls=%async_computation.3 | async-start | bytes 2621440 | tf_op jit(solution)/shard_map/all_gather | solution.py:453
  26.8 36.6 %collective-permute-start.19 = (bf16[5,5,64,256]{3,2,1,0:T(8,128)(2,1)}, bf16[5,5,64,256]{3,2,1,0:T(8,128)(2,1)S(1)}, u32[]{:S(2)}, u32[]{:S(2)}) collective-permute-start(bf16[5,5,64,256]{3,2,1,0:T(8,128)(2,1)} %bitcast.170), channel_id=1, source_target_pairs={{0,12},{4,8},{8,4},{12,0},{1,13},{5,9},{9,5},{13,1},{2,14},{6,10},... | collective-permute-start | bytes 2457608 | tf_op jit(solution)/shard_map/ppermute | solution.py:271
  66.5 32.5 %collective-permute-start.22 = (bf16[5,8,64,256]{3,2,1,0:T(8,128)(2,1)}, bf16[5,8,64,256]{3,2,1,0:T(8,128)(2,1)}, u32[]{:S(2)}, u32[]{:S(2)}) collective-permute-start(bf16[5,8,64,256]{3,2,1,0:T(8,128)(2,1)} %get-tuple-element.8103), channel_id=1, source_target_pairs={{0,3},{1,2},{2,1},{3,0},{4,7},{5,6},{6,5},{7,4},{8,11},{9,10},{10,... | collective-permute-start | bytes 3932168 | tf_op jit(solution)/shard_map/ppermute | solution.py:271
  69.9 112.3 %collective-permute-start.21 = (bf16[5,8,64,256]{3,2,1,0:T(8,128)(2,1)}, bf16[5,8,64,256]{3,2,1,0:T(8,128)(2,1)}, u32[]{:S(2)}, u32[]{:S(2)}) collective-permute-start(bf16[5,8,64,256]{3,2,1,0:T(8,128)(2,1)} %get-tuple-element.8104), channel_id=1, source_target_pairs={{0,2},{1,3},{2,0},{3,1},{4,6},{5,7},{6,4},{7,5},{8,10},{9,11},{10,... | collective-permute-start | bytes 3932168 | tf_op jit(solution)/shard_map/ppermute | solution.py:271
  69.9 112.3 %collective-permute-start.20 = (bf16[5,8,64,256]{3,2,1,0:T(8,128)(2,1)}, bf16[5,8,64,256]{3,2,1,0:T(8,128)(2,1)}, u32[]{:S(2)}, u32[]{:S(2)}) collective-permute-start(bf16[5,8,64,256]{3,2,1,0:T(8,128)(2,1)} %get-tuple-element.8105), channel_id=1, source_target_pairs={{0,1},{1,0},{2,3},{3,2},{4,5},{5,4},{6,7},{7,6},{8,9},{9,8},{10,11... | collective-permute-start | bytes 3932168 | tf_op jit(solution)/shard_map/ppermute | solution.py:271
  73.2 109.0 %collective-permute-start.16 = (bf16[1024,512]{1,0:T(8,128)(2,1)}, bf16[1024,512]{1,0:T(8,128)(2,1)S(1)}, u32[]{:S(2)}, u32[]{:S(2)}) collective-permute-start(bf16[1024,512]{1,0:T(8,128)(2,1)} %get-tuple-element.8155), channel_id=1, source_target_pairs={{0,8},{4,12},{9,1},{13,5},{18,26},{22,30},{27,19},{31,23}} | collective-permute-start | bytes 3145736 | tf_op jit(solution)/shard_map/ppermute | solution.py:471
  74.5 107.8 %collective-permute-start.15 = (bf16[1024,512]{1,0:T(8,128)(2,1)}, bf16[1024,512]{1,0:T(8,128)(2,1)S(1)}, u32[]{:S(2)}, u32[]{:S(2)}) collective-permute-start(bf16[1024,512]{1,0:T(8,128)(2,1)} %get-tuple-element.8156), channel_id=1, source_target_pairs={{0,16},{4,20},{9,25},{13,29},{18,2},{22,6},{27,11},{31,15}} | collective-permute-start | bytes 3145736 | tf_op jit(solution)/shard_map/ppermute | solution.py:471
  182.3 158.7 %all-gather.15.cloned.1.call-start = ((), (), s32[]{:S(2)}) async-start(), calls=%async_computation.4 | async-start | bytes 2621440 | tf_op jit(solution)/shard_map/all_gather | solution.py:453
  183.0 173.3 %all-gather.9.cloned.1.call-start = ((), (), s32[]{:S(2)}) async-start(), calls=%async_computation.1 | async-start | bytes 2621440 | tf_op jit(solution)/shard_map/all_gather | solution.py:453
  206.7 51.9 %collective-permute-start.26 = (bf16[18,4,64,256]{3,2,1,0:T(8,128)(2,1)}, bf16[18,4,64,256]{3,2,1,0:T(8,128)(2,1)}, u32[]{:S(2)}, u32[]{:S(2)}) collective-permute-start(bf16[18,4,64,256]{3,2,1,0:T(8,128)(2,1)} %pad_maximum_fusion.19), channel_id=1, source_target_pairs={{0,8},{4,12},{8,0},{12,4},{1,9},{5,13},{9,1},{13,5},{2,10},{6,14},... | collective-permute-start | bytes 7077896 | tf_op jit(solution)/shard_map/ppermute | solution.py:271
  211.4 43.2 %collective-permute-start.25 = (bf16[15,4,64,256]{3,2,1,0:T(8,128)(2,1)}, bf16[15,4,64,256]{3,2,1,0:T(8,128)(2,1)}, u32[]{:S(2)}, u32[]{:S(2)}) collective-permute-start(bf16[15,4,64,256]{3,2,1,0:T(8,128)(2,1)} %get-tuple-element.8111), channel_id=1, source_target_pairs={{0,16},{16,0},{1,17},{17,1},{2,18},{18,2},{3,19},{19,3},{4,20},{20... | collective-permute-start | bytes 5898248 | tf_op jit(solution)/shard_map/ppermute | solution.py:271
  212.8 180.3 %all-gather.11.cloned.1.call-start = ((), (), s32[]{:S(2)}) async-start(), calls=%async_computation.2 | async-start | bytes 2621440 | tf_op jit(solution)/shard_map/all_gather | solution.py:453
  232.6 48.5 %collective-permute-start.24 = (bf16[1024,512]{1,0:T(8,128)(2,1)}, bf16[1024,512]{1,0:T(8,128)(2,1)}, u32[]{:S(2)}, u32[]{:S(2)}) collective-permute-start(bf16[1024,512]{1,0:T(8,128)(2,1)} %get-tuple-element.8153), channel_id=1, source_target_pairs={{0,8},{4,12},{9,1},{13,5},{18,26},{22,30},{27,19},{31,23},{8,24},{... | collective-permute-start | bytes 3145736 | tf_op jit(solution)/shard_map/ppermute | solution.py:471
  235.7 45.5 %collective-permute-start.23 = (bf16[1024,512]{1,0:T(8,128)(2,1)}, bf16[1024,512]{1,0:T(8,128)(2,1)}, u32[]{:S(2)}, u32[]{:S(2)}) collective-permute-start(bf16[1024,512]{1,0:T(8,128)(2,1)} %get-tuple-element.8154), channel_id=1, source_target_pairs={{0,16},{4,20},{9,25},{13,29},{18,2},{22,6},{27,11},{31,15},{16,24}... | collective-permute-start | bytes 3145736 | tf_op jit(solution)/shard_map/ppermute | solution.py:471
  286.1 51.0 %collective-permute-start.28 = (bf16[18,4,64,256]{3,2,1,0:T(8,128)(2,1)}, bf16[18,4,64,256]{3,2,1,0:T(8,128)(2,1)}, u32[]{:S(2)}, u32[]{:S(2)}) collective-permute-start(bf16[18,4,64,256]{3,2,1,0:T(8,128)(2,1)} %pad_maximum_fusion.22), channel_id=1, source_target_pairs={{0,16},{16,0},{1,17},{17,1},{2,18},{18,2},{3,19},{19,3},{4,20},{20... | collective-permute-start | bytes 7077896 | tf_op jit(solution)/shard_map/ppermute | solution.py:271
  294.6 50.7 %collective-permute-start.27 = (bf16[18,4,64,256]{3,2,1,0:T(8,128)(2,1)}, bf16[18,4,64,256]{3,2,1,0:T(8,128)(2,1)}, u32[]{:S(2)}, u32[]{:S(2)}) collective-permute-start(bf16[18,4,64,256]{3,2,1,0:T(8,128)(2,1)} %pad_maximum_fusion.21), channel_id=1, source_target_pairs={{0,8},{4,12},{8,0},{12,4},{1,9},{5,13},{9,1},{13,5},{2,10},{6,14},... | collective-permute-start | bytes 7077896 | tf_op jit(solution)/shard_map/ppermute | solution.py:271
  294.6 172.9 %all-gather.17.cloned.1.call-start = ((), (), s32[]{:S(2)}) async-start(), calls=%async_computation.5 | async-start | bytes 2621440 | tf_op jit(solution)/shard_map/all_gather | solution.py:453
  349.0 23.6 %collective-permute-start.30 = (bf16[1024,512]{1,0:T(8,128)(2,1)}, bf16[1024,512]{1,0:T(8,128)(2,1)S(1)}, u32[]{:S(2)}, u32[]{:S(2)}) collective-permute-start(bf16[1024,512]{1,0:T(8,128)(2,1)} %get-tuple-element.8151), channel_id=1, source_target_pairs={{0,8},{4,12},{9,1},{13,5},{18,26},{22,30},{27,19},{31,23},{8,24},{... | collective-permute-start | bytes 3145736 | tf_op jit(solution)/shard_map/ppermute | solution.py:471
  384.4 35.5 %collective-permute-start.36 = (bf16[24,4,64,256]{3,2,1,0:T(8,128)(2,1)}, bf16[24,4,64,256]{3,2,1,0:T(8,128)(2,1)S(1)}, u32[]{:S(2)}, u32[]{:S(2)}) collective-permute-start(bf16[24,4,64,256]{3,2,1,0:T(8,128)(2,1)} %pad_maximum_fusion.17), channel_id=1, source_target_pairs={{0,4},{4,0},{8,12},{12,8},{1,5},{5,1},{9,13},{13,9},{2,6},{6,2},{1... | collective-permute-start | bytes 9437192 | tf_op jit(solution)/shard_map/ppermute | solution.py:271
  392.2 48.0 %collective-permute-start.35 = (bf16[24,4,64,256]{3,2,1,0:T(8,128)(2,1)}, bf16[24,4,64,256]{3,2,1,0:T(8,128)(2,1)}, u32[]{:S(2)}, u32[]{:S(2)}) collective-permute-start(bf16[24,4,64,256]{3,2,1,0:T(8,128)(2,1)} %pad_maximum_fusion.16), channel_id=1, source_target_pairs={{0,4},{4,0},{8,12},{12,8},{1,5},{5,1},{9,13},{13,9},{2,6},{6,2},{1... | collective-permute-start | bytes 9437192 | tf_op jit(solution)/shard_map/ppermute | solution.py:271
  411.4 56.0 %collective-permute-start.38 = (bf16[2048,512]{1,0:T(8,128)(2,1)}, bf16[2048,512]{1,0:T(8,128)(2,1)}, u32[]{:S(2)}, u32[]{:S(2)}) collective-permute-start(bf16[2048,512]{1,0:T(8,128)(2,1)} %pad_maximum_fusion.26.refs_3_), channel_id=1, source_target_pairs={{0,4},{4,0},{8,12},{12,8},{1,5},{5,1},{9,13},{13,9},{2,6},{6,2},{1... | collective-permute-start | bytes 6291464 | tf_op jit(solution)/shard_map/ppermute | solution.py:271
  418.0 49.5 %collective-permute-start.37 = (bf16[2048,512]{1,0:T(8,128)(2,1)}, bf16[2048,512]{1,0:T(8,128)(2,1)}, u32[]{:S(2)}, u32[]{:S(2)}) collective-permute-start(bf16[2048,512]{1,0:T(8,128)(2,1)} %pad_maximum_fusion.25.refs_2_), channel_id=1, source_target_pairs={{0,4},{4,0},{8,12},{12,8},{1,5},{5,1},{9,13},{13,9},{2,6},{6,2},{1... | collective-permute-start | bytes 6291464 | tf_op jit(solution)/shard_map/ppermute | solution.py:271
  418.0 49.5 %collective-permute-start.34 = (bf16[1024,512]{1,0:T(8,128)(2,1)}, bf16[1024,512]{1,0:T(8,128)(2,1)}, u32[]{:S(2)}, u32[]{:S(2)}) collective-permute-start(bf16[1024,512]{1,0:T(8,128)(2,1)} %get-tuple-element.8143), channel_id=1, source_target_pairs={{0,8},{4,12},{9,1},{13,5},{18,26},{22,30},{27,19},{31,23},{8,24},{... | collective-permute-start | bytes 3145736 | tf_op jit(solution)/shard_map/ppermute | solution.py:471
  419.9 47.6 %collective-permute-start.33 = (bf16[1024,512]{1,0:T(8,128)(2,1)}, bf16[1024,512]{1,0:T(8,128)(2,1)}, u32[]{:S(2)}, u32[]{:S(2)}) collective-permute-start(bf16[1024,512]{1,0:T(8,128)(2,1)} %get-tuple-element.8144), channel_id=1, source_target_pairs={{0,16},{4,20},{9,25},{13,29},{18,2},{22,6},{27,11},{31,15},{16,24}... | collective-permute-start | bytes 3145736 | tf_op jit(solution)/shard_map/ppermute | solution.py:471
  472.4 82.9 %collective-permute-start.45 = (bf16[1024,512]{1,0:T(8,128)(2,1)}, bf16[1024,512]{1,0:T(8,128)(2,1)}, u32[]{:S(2)}, u32[]{:S(2)}) collective-permute-start(bf16[1024,512]{1,0:T(8,128)(2,1)} %get-tuple-element.8133), channel_id=1, source_target_pairs={{0,16},{4,20},{9,25},{13,29},{18,2},{22,6},{27,11},{31,15}} | collective-permute-start | bytes 3145736 | tf_op jit(solution)/shard_map/ppermute | solution.py:471
  475.5 44.3 %collective-permute-start.41 = (bf16[2048,512]{1,0:T(8,128)(2,1)}, bf16[2048,512]{1,0:T(8,128)(2,1)}, u32[]{:S(2)}, u32[]{:S(2)}) collective-permute-start(bf16[2048,512]{1,0:T(8,128)(2,1)} %pad_maximum_fusion.27.refs_1_), channel_id=1, source_target_pairs={{0,4},{4,0},{8,12},{12,8},{1,5},{5,1},{9,13},{13,9},{2,6},{6,2},{1... | collective-permute-start | bytes 6291464 | tf_op jit(solution)/shard_map/ppermute | solution.py:271
  476.5 43.2 %collective-permute-start.39 = (bf16[1024,512]{1,0:T(8,128)(2,1)}, bf16[1024,512]{1,0:T(8,128)(2,1)S(1)}, u32[]{:S(2)}, u32[]{:S(2)}) collective-permute-start(bf16[1024,512]{1,0:T(8,128)(2,1)} %get-tuple-element.8134), channel_id=1, source_target_pairs={{0,16},{4,20},{9,25},{13,29},{18,2},{22,6},{27,11},{31,15},{16,24}... | collective-permute-start | bytes 3145736 | tf_op jit(solution)/shard_map/ppermute | solution.py:471
  477.8 41.9 %collective-permute-start.40 = (bf16[1024,512]{1,0:T(8,128)(2,1)}, bf16[1024,512]{1,0:T(8,128)(2,1)}, u32[]{:S(2)}, u32[]{:S(2)}) collective-permute-start(bf16[1024,512]{1,0:T(8,128)(2,1)} %get-tuple-element.8135), channel_id=1, source_target_pairs={{0,8},{4,12},{9,1},{13,5},{18,26},{22,30},{27,19},{31,23},{8,24},{... | collective-permute-start | bytes 3145736 | tf_op jit(solution)/shard_map/ppermute | solution.py:471
  483.8 71.5 %collective-permute-start.44 = (bf16[1024,512]{1,0:T(8,128)(2,1)}, bf16[1024,512]{1,0:T(8,128)(2,1)}, u32[]{:S(2)}, u32[]{:S(2)}) collective-permute-start(bf16[1024,512]{1,0:T(8,128)(2,1)} %get-tuple-element.8136), channel_id=1, source_target_pairs={{0,8},{4,12},{9,1},{13,5},{18,26},{22,30},{27,19},{31,23}} | collective-permute-start | bytes 3145736 | tf_op jit(solution)/shard_map/ppermute | solution.py:471
  519.7 35.5 %collective-permute-start.42 = (bf16[1024,512]{1,0:T(8,128)(2,1)S(1)}, bf16[1024,512]{1,0:T(8,128)(2,1)}, u32[]{:S(2)}, u32[]{:S(2)}) collective-permute-start(bf16[1024,512]{1,0:T(8,128)(2,1)S(1)} %collective-permute-done.39), channel_id=1, source_target_pairs={{16,24},{20,28},{25,17},{29,21},{2,10},{6,14},{11,3},{15,7},{24,8}... | collective-permute-start | bytes 3145736 | tf_op jit(solution)/shard_map/ppermute | solution.py:471
  521.3 34.0 %collective-permute-start.43 = (bf16[1024,512]{1,0:T(8,128)(2,1)}, bf16[1024,512]{1,0:T(8,128)(2,1)}, u32[]{:S(2)}, u32[]{:S(2)}) collective-permute-start(bf16[1024,512]{1,0:T(8,128)(2,1)} %collective-permute-done.40), channel_id=1, source_target_pairs={{8,24},{12,28},{1,17},{5,21},{26,10},{30,14},{19,3},{23,7},{24,16}... | collective-permute-start | bytes 3145736 | tf_op jit(solution)/shard_map/ppermute | solution.py:471
  (37 other events, 532.5 us)
Sparse Core Ops, SparseCore 0:
  13.3 47.1 all-gather.6
  182.4 46.4 all-gather.12
  230.5 44.6 all-gather.14
  276.6 44.6 all-gather.8
  322.7 44.6 all-gather.10
  368.8 44.6 all-gather.16

commit v3 on v2

--- a/solution.py
+++ b/solution.py
@@ -532,9 +532,9 @@
     got = beat(2, got)
     far = third_rows(near, row_turns)
     base = extend(front_trailing, near, far, tables, False)
-    got = beat(4, beat(3, got))
-    columns = [columns_of(c, got) for c in (0, 1)]
-    got, base, columns, row_chunks[5] = fence((got, base, columns, row_chunks[5]))
+    got = beat(3, got)
+    columns = [columns_of(0, got)]
+    got, base, columns, row_chunks[4] = fence((got, base, columns, row_chunks[4]))
 
     row_rounds = [rounds_of(edges, size) for edges, size in zip(row_edges, row_windows)]
     every_round = functools.reduce(lambda a, b: a * b, row_rounds)
@@ -559,12 +559,13 @@
     left = jnp.maximum(most - col_window, 0)
     base = lax.fori_loop(0, (left + MORE_COLUMNS - 1) // MORE_COLUMNS, more_columns, base)
 
-    base = subtract(base, 0, columns)
-    columns = [columns_of(2, got)]
+    columns.append(columns_of(1, got))
+    got = beat(4, got)
+    columns.append(columns_of(2, got))
     got = beat(5, got)
     got, base, columns = fence((got, base, columns))
 
-    base = subtract(base, 2, columns)
+    base = subtract(base, 0, columns)
     straight = [hand_on(held, [(0, way[3])]) for held, way in zip(halves_of(5), ring)]
     got = beat(6, got)
 

time: 628 us -> 614 us (0.978)
  Pallas kernels: 134 us -> 111 us
    pallas_call x3 -> x2, Pallas kernels: 101 us -> 77.3 us  [update(): pl.pallas_call(functools.partial(update_kernel, tile, len(rows)), grid_sp...]
    ppermute x16, waiting for transfers between devices: 51.1 us -> 59.2 us  [hand_on(): return lax.ppermute(held, ('sub', 'row', 'col'), pairs)]
    ppermute x18, waiting for transfers between devices: 189 us -> 182 us  [xor_permute(): return lax.ppermute(value, axes, [(i, i ^ mask) for i in range(size)])]
  transfers between devices with their start and end apart: 40 -> 40, of which waited for: 16 -> 17; matrix products, arithmetic and copies ran while one was open for 16% -> 18% of each run, Pallas kernels for 15% -> 11%
where the time goes in v3:
time: 614 us; the launch traced here: 605 us
  waiting for transfers between devices  258 us (42%)
  Pallas kernels  111 us (18%)
  local copies, waits for them, and re-layouts  63.7 us (10%)
  between operations  58 us (9%)
  starting transfers between devices  57.4 us (9%)
  other arithmetic  56.1 us (9%)
    ppermute x18, waiting for transfers between devices, xor_permute(): return lax.ppermute(value, axes, [(i, i ^ mask) for i in range(size)])  182 us
    pallas_call x2, Pallas kernels, update(): pl.pallas_call(functools.partial(update_kernel, tile, len(rows)), grid_sp...  77.3 us
    ppermute x16, waiting for transfers between devices, hand_on(): return lax.ppermute(held, ('sub', 'row', 'col'), pairs)  59.2 us
    ppermute x16, starting transfers between devices, hand_on(): return lax.ppermute(held, ('sub', 'row', 'col'), pairs)  37.4 us
    pallas_call x1, Pallas kernels, extend_add(): pl.pallas_call(functools.partial(extend_kernel, tile, parts, groups), gri...  27.8 us
    ppermute x18, starting transfers between devices, xor_permute(): return lax.ppermute(value, axes, [(i, i ^ mask) for i in range(size)])  19.8 us
    dynamic_slice x10, local copies, waits for them, and re-layouts, taken(): return lax.dynamic_slice_in_dim(value, start, size, 0)  19 us
    all_gather x6, waiting for transfers between devices, gather(): lax.all_gather(piece, 'col', axis=0, tiled=True)  16.4 us
  transfers between devices with their start and end apart: 40, of which 17 were waited for; matrix products, arithmetic and copies ran while one was open for 18% of the time, Pallas kernels for 11%

profile of v3, /device:TPU:5, one launch (start us, length us, event | category | flops | bytes accessed | tf_op | source)
XLA Modules:
  0.0 604.8 jit_solution(9658303468425613772)
XLA Ops:
  7.2 6.0 shard_map.77
  13.3 5.6 reshape.992
  18.9 3.9 constant_dynamic-slice_fusion.56
  34.2 11.7 %collective-permute-done.18 = bf16[5,5,64,256]{3,2,1,0:T(8,128)(2,1)S(1)} collective-permute-done((bf16[5,5,64,256]{3,2,1,0:T(8,128)(2,1)}, bf16[5,5,64,256]{3,2,1,0:T(8,128)(2,1)S(1)}, u32[]{:S(2)}, u32[]{:S(2)}) %collective-permute-start.18) | collective-permute-done | bytes 819232 | tf_op jit(solution)/shard_map/ppermute | solution.py:271
  45.9 17.5 %collective-permute-done.19 = bf16[5,5,64,256]{3,2,1,0:T(8,128)(2,1)S(1)} collective-permute-done((bf16[5,5,64,256]{3,2,1,0:T(8,128)(2,1)}, bf16[5,5,64,256]{3,2,1,0:T(8,128)(2,1)S(1)}, u32[]{:S(2)}, u32[]{:S(2)}) %collective-permute-start.19) | collective-permute-done | bytes 819232 | tf_op jit(solution)/shard_map/ppermute | solution.py:271
  90.1 3.9 select_bitcast_fusion.12
  99.1 83.2 %collective-permute-done.21 = bf16[5,8,64,256]{3,2,1,0:T(8,128)(2,1)} collective-permute-done((bf16[5,8,64,256]{3,2,1,0:T(8,128)(2,1)}, bf16[5,8,64,256]{3,2,1,0:T(8,128)(2,1)}, u32[]{:S(2)}, u32[]{:S(2)}) %collective-permute-start.21) | collective-permute-done | bytes 1310752 | tf_op jit(solution)/shard_map/ppermute | solution.py:271
  200.6 4.6 constant_dynamic-slice_fusion.45
  207.5 3.9 constant_dynamic-slice_fusion.48
  212.6 16.4 %all-gather.11.cloned.1.call-done.refs_1_ = bf16[2048,512]{1,0:T(8,128)(2,1)} async-done(((bf16[512,512]{1,0:T(8,128)(2,1)}), bf16[2048,512]{1,0:T(8,128)(2,1)}) %all-gather.11.cloned.1.call-update) | async-done | bytes 2097168 | tf_op jit(solution)/shard_map/all_gather | solution.py:453
  239.2 15.4 %collective-permute-done.25 = bf16[15,4,64,256]{3,2,1,0:T(8,128)(2,1)} collective-permute-done((bf16[15,4,64,256]{3,2,1,0:T(8,128)(2,1)}, bf16[15,4,64,256]{3,2,1,0:T(8,128)(2,1)}, u32[]{:S(2)}, u32[]{:S(2)}) %collective-permute-start.25) | collective-permute-done | bytes 1966112 | tf_op jit(solution)/shard_map/ppermute | solution.py:271
  254.6 4.1 collective-permute-done.26
  258.7 22.4 %collective-permute-done.24 = bf16[1024,512]{1,0:T(8,128)(2,1)S(1)} collective-permute-done((bf16[1024,512]{1,0:T(8,128)(2,1)}, bf16[1024,512]{1,0:T(8,128)(2,1)S(1)}, u32[]{:S(2)}, u32[]{:S(2)}) %collective-permute-start.24) | collective-permute-done | bytes 1048608 | tf_op jit(solution)/shard_map/ppermute | solution.py:471
  302.4 35.9 %collective-permute-done.28 = bf16[18,4,64,256]{3,2,1,0:T(8,128)(2,1)} collective-permute-done((bf16[18,4,64,256]{3,2,1,0:T(8,128)(2,1)}, bf16[18,4,64,256]{3,2,1,0:T(8,128)(2,1)}, u32[]{:S(2)}, u32[]{:S(2)}) %collective-permute-start.28) | collective-permute-done | bytes 2359328 | tf_op jit(solution)/shard_map/ppermute | solution.py:271
  343.4 4.1 collective-permute-done.27.refs_2_.refs_6_
  360.2 3.5 collective-permute-start.34
  365.7 9.1 %collective-permute-done.30 = bf16[1024,512]{1,0:T(8,128)(2,1)} collective-permute-done((bf16[1024,512]{1,0:T(8,128)(2,1)}, bf16[1024,512]{1,0:T(8,128)(2,1)}, u32[]{:S(2)}, u32[]{:S(2)}) %collective-permute-start.30) | collective-permute-done | bytes 1048608 | tf_op jit(solution)/shard_map/ppermute | solution.py:471
  376.8 4.4 broadcast_select_fusion.4
  382.5 4.4 collective-permute-start.35
  392.6 27.8 %shard_map.78 = f32[2048,4096]{1,0:T(8,128)} custom-call(s32[8,8]{1,0:T(8,128)} %stack.40.row_at, s32[2,8]{1,0:T(2,128)} %pad_add_fusion.2.col_at, s32[1]{0:T(128)} %bitcast.93.me, f32[2048,4096]{1,0:T(8,128)} %base_ref.1, bf16[18,4,64,256]{3,2,1,0:T(8,128)(2,1)} %copy-done.31, ...), custom_call_target="tpu_custom_call" | custom-call | flops 8388608 | bytes 67108864 | tf_op jit(solution)/shard_map/pallas_call | solution.py:183
  420.4 3.8 broadcast_select_fusion.2
  424.3 5.6 collective-permute-start.37
  452.6 4.1 collective-permute-done.36
  456.7 4.1 select_select_fusion.7
  464.2 3.6 fusion.25
  470.2 4.0 collective-permute-start.39
  475.9 19.6 %collective-permute-done.38 = bf16[1024,512]{1,0:T(8,128)(2,1)S(1)} collective-permute-done((bf16[1024,512]{1,0:T(8,128)(2,1)}, bf16[1024,512]{1,0:T(8,128)(2,1)S(1)}, u32[]{:S(2)}, u32[]{:S(2)}) %collective-permute-start.38) | collective-permute-done | bytes 1048608 | tf_op jit(solution)/shard_map/ppermute | solution.py:471
  498.1 5.4 collective-permute-start.43
  503.6 38.8 %shard_map.79.refs_9_ = f32[2048,4096]{1,0:T(8,128)} custom-call(s32[1]{0:T(128)} %bitcast.51.core, s32[8,16]{1,0:T(8,128)} %dynamic_slice.1092.mask, bf16[2048,512]{1,0:T(8,128)(2,1)} %all-gather.7.cloned.1.call-done.refs_0_, bf16[2048,512]{1,0:T(8,128)(2,1)} %all-gather.11.cloned.1.call-done.refs_1_, ...), custom_call_target="tpu_custom_call", output_to_operand_aliasing={{}: (11, {})} | custom-call | flops 25769803776 | bytes 67108864 | tf_op jit(solution)/shard_map/pallas_call | solution.py:251
  542.5 3.6 select_select_fusion.1
  551.9 6.0 collective-permute-done.47.refs_7_
  559.3 38.5 %shard_map.80 = f32[2048,4096]{1,0:T(8,128)} custom-call(s32[1]{0:T(128)} %bitcast.51.core, s32[8,16]{1,0:T(8,128)} %dynamic_slice.1092.mask, bf16[2048,512]{1,0:T(8,128)(2,1)} %all-gather.9.cloned.1.call-done.refs_0_, bf16[2048,512]{1,0:T(8,128)(2,1)} %all-gather.15.cloned.1.call-done.refs_1_, ...), custom_call_target="tpu_custom_call", output_to_operand_aliasing={{}: (11, {})} | custom-call | flops 25769803776 | bytes 67108864 | tf_op jit(solution)/shard_map/pallas_call | solution.py:251
  (197 shorter events, 122.2 us)
Async XLA Ops:
  7.2 63.1 %all-gather.7.cloned.1.call-start = ((), (), s32[]{:S(2)}) async-start(), calls=%async_computation | async-start | bytes 2621440 | tf_op jit(solution)/shard_map/all_gather | solution.py:453
  13.2 215.7 %all-gather.11.cloned.1.call-start = ((), (), s32[]{:S(2)}) async-start(), calls=%async_computation.2 | async-start | bytes 2621440 | tf_op jit(solution)/shard_map/all_gather | solution.py:453
  26.8 36.6 %collective-permute-start.19 = (bf16[5,5,64,256]{3,2,1,0:T(8,128)(2,1)}, bf16[5,5,64,256]{3,2,1,0:T(8,128)(2,1)S(1)}, u32[]{:S(2)}, u32[]{:S(2)}) collective-permute-start(bf16[5,5,64,256]{3,2,1,0:T(8,128)(2,1)} %bitcast.170), channel_id=1, source_target_pairs={{0,12},{4,8},{8,4},{12,0},{1,13},{5,9},{9,5},{13,1},{2,14},{6,10},... | collective-permute-start | bytes 2457608 | tf_op jit(solution)/shard_map/ppermute | solution.py:271
  66.6 32.5 %collective-permute-start.22 = (bf16[5,8,64,256]{3,2,1,0:T(8,128)(2,1)}, bf16[5,8,64,256]{3,2,1,0:T(8,128)(2,1)}, u32[]{:S(2)}, u32[]{:S(2)}) collective-permute-start(bf16[5,8,64,256]{3,2,1,0:T(8,128)(2,1)} %get-tuple-element.8107), channel_id=1, source_target_pairs={{0,3},{1,2},{2,1},{3,0},{4,7},{5,6},{6,5},{7,4},{8,11},{9,10},{10,... | collective-permute-start | bytes 3932168 | tf_op jit(solution)/shard_map/ppermute | solution.py:271
  70.0 112.3 %collective-permute-start.21 = (bf16[5,8,64,256]{3,2,1,0:T(8,128)(2,1)}, bf16[5,8,64,256]{3,2,1,0:T(8,128)(2,1)}, u32[]{:S(2)}, u32[]{:S(2)}) collective-permute-start(bf16[5,8,64,256]{3,2,1,0:T(8,128)(2,1)} %get-tuple-element.8108), channel_id=1, source_target_pairs={{0,2},{1,3},{2,0},{3,1},{4,6},{5,7},{6,4},{7,5},{8,10},{9,11},{10,... | collective-permute-start | bytes 3932168 | tf_op jit(solution)/shard_map/ppermute | solution.py:271
  70.0 112.3 %collective-permute-start.20 = (bf16[5,8,64,256]{3,2,1,0:T(8,128)(2,1)}, bf16[5,8,64,256]{3,2,1,0:T(8,128)(2,1)}, u32[]{:S(2)}, u32[]{:S(2)}) collective-permute-start(bf16[5,8,64,256]{3,2,1,0:T(8,128)(2,1)} %get-tuple-element.8109), channel_id=1, source_target_pairs={{0,1},{1,0},{2,3},{3,2},{4,5},{5,4},{6,7},{7,6},{8,9},{9,8},{10,11... | collective-permute-start | bytes 3932168 | tf_op jit(solution)/shard_map/ppermute | solution.py:271
  73.3 109.0 %collective-permute-start.16 = (bf16[1024,512]{1,0:T(8,128)(2,1)}, bf16[1024,512]{1,0:T(8,128)(2,1)S(1)}, u32[]{:S(2)}, u32[]{:S(2)}) collective-permute-start(bf16[1024,512]{1,0:T(8,128)(2,1)} %get-tuple-element.8157), channel_id=1, source_target_pairs={{0,8},{4,12},{9,1},{13,5},{18,26},{22,30},{27,19},{31,23}} | collective-permute-start | bytes 3145736 | tf_op jit(solution)/shard_map/ppermute | solution.py:471
  74.5 107.7 %collective-permute-start.15 = (bf16[1024,512]{1,0:T(8,128)(2,1)}, bf16[1024,512]{1,0:T(8,128)(2,1)}, u32[]{:S(2)}, u32[]{:S(2)}) collective-permute-start(bf16[1024,512]{1,0:T(8,128)(2,1)} %get-tuple-element.8158), channel_id=1, source_target_pairs={{0,16},{4,20},{9,25},{13,29},{18,2},{22,6},{27,11},{31,15}} | collective-permute-start | bytes 3145736 | tf_op jit(solution)/shard_map/ppermute | solution.py:471
  182.3 161.1 %all-gather.13.cloned.1.call-start = ((), (), s32[]{:S(2)}) async-start(), calls=%async_computation.3 | async-start | bytes 2621440 | tf_op jit(solution)/shard_map/all_gather | solution.py:453
  187.5 178.2 %all-gather.9.cloned.1.call-start = ((), (), s32[]{:S(2)}) async-start(), calls=%async_computation.1 | async-start | bytes 2621440 | tf_op jit(solution)/shard_map/all_gather | solution.py:453
  206.7 52.0 %collective-permute-start.26 = (bf16[18,4,64,256]{3,2,1,0:T(8,128)(2,1)}, bf16[18,4,64,256]{3,2,1,0:T(8,128)(2,1)}, u32[]{:S(2)}, u32[]{:S(2)}) collective-permute-start(bf16[18,4,64,256]{3,2,1,0:T(8,128)(2,1)} %pad_maximum_fusion.19), channel_id=1, source_target_pairs={{0,8},{4,12},{8,0},{12,4},{1,9},{5,13},{9,1},{13,5},{2,10},{6,14},... | collective-permute-start | bytes 7077896 | tf_op jit(solution)/shard_map/ppermute | solution.py:271
  211.3 43.3 %collective-permute-start.25 = (bf16[15,4,64,256]{3,2,1,0:T(8,128)(2,1)}, bf16[15,4,64,256]{3,2,1,0:T(8,128)(2,1)}, u32[]{:S(2)}, u32[]{:S(2)}) collective-permute-start(bf16[15,4,64,256]{3,2,1,0:T(8,128)(2,1)} %get-tuple-element.8115), channel_id=1, source_target_pairs={{0,16},{16,0},{1,17},{17,1},{2,18},{18,2},{3,19},{19,3},{4,20},{20... | collective-permute-start | bytes 5898248 | tf_op jit(solution)/shard_map/ppermute | solution.py:271
  232.4 48.7 %collective-permute-start.24 = (bf16[1024,512]{1,0:T(8,128)(2,1)}, bf16[1024,512]{1,0:T(8,128)(2,1)S(1)}, u32[]{:S(2)}, u32[]{:S(2)}) collective-permute-start(bf16[1024,512]{1,0:T(8,128)(2,1)} %get-tuple-element.8155), channel_id=1, source_target_pairs={{0,8},{4,12},{9,1},{13,5},{18,26},{22,30},{27,19},{31,23},{8,24},{... | collective-permute-start | bytes 3145736 | tf_op jit(solution)/shard_map/ppermute | solution.py:471
  235.5 45.6 %collective-permute-start.23 = (bf16[1024,512]{1,0:T(8,128)(2,1)}, bf16[1024,512]{1,0:T(8,128)(2,1)}, u32[]{:S(2)}, u32[]{:S(2)}) collective-permute-start(bf16[1024,512]{1,0:T(8,128)(2,1)} %get-tuple-element.8156), channel_id=1, source_target_pairs={{0,16},{4,20},{9,25},{13,29},{18,2},{22,6},{27,11},{31,15},{16,24}... | collective-permute-start | bytes 3145736 | tf_op jit(solution)/shard_map/ppermute | solution.py:471
  237.2 183.2 %all-gather.15.cloned.1.call-start = ((), (), s32[]{:S(2)}) async-start(), calls=%async_computation.4 | async-start | bytes 2621440 | tf_op jit(solution)/shard_map/all_gather | solution.py:453
  287.2 51.1 %collective-permute-start.28 = (bf16[18,4,64,256]{3,2,1,0:T(8,128)(2,1)}, bf16[18,4,64,256]{3,2,1,0:T(8,128)(2,1)}, u32[]{:S(2)}, u32[]{:S(2)}) collective-permute-start(bf16[18,4,64,256]{3,2,1,0:T(8,128)(2,1)} %pad_maximum_fusion.22), channel_id=1, source_target_pairs={{0,16},{16,0},{1,17},{17,1},{2,18},{18,2},{3,19},{19,3},{4,20},{20... | collective-permute-start | bytes 7077896 | tf_op jit(solution)/shard_map/ppermute | solution.py:271
  296.7 50.8 %collective-permute-start.27 = (bf16[18,4,64,256]{3,2,1,0:T(8,128)(2,1)}, bf16[18,4,64,256]{3,2,1,0:T(8,128)(2,1)}, u32[]{:S(2)}, u32[]{:S(2)}) collective-permute-start(bf16[18,4,64,256]{3,2,1,0:T(8,128)(2,1)} %pad_maximum_fusion.21), channel_id=1, source_target_pairs={{0,8},{4,12},{8,0},{12,4},{1,9},{5,13},{9,1},{13,5},{2,10},{6,14},... | collective-permute-start | bytes 7077896 | tf_op jit(solution)/shard_map/ppermute | solution.py:271
  300.5 163.7 %all-gather.17.cloned.1.call-start = ((), (), s32[]{:S(2)}) async-start(), calls=%async_computation.5 | async-start | bytes 2621440 | tf_op jit(solution)/shard_map/all_gather | solution.py:453
  360.2 30.6 %collective-permute-start.34 = (bf16[24,4,64,256]{3,2,1,0:T(8,128)(2,1)}, bf16[24,4,64,256]{3,2,1,0:T(8,128)(2,1)S(1)}, u32[]{:S(2)}, u32[]{:S(2)}) collective-permute-start(bf16[24,4,64,256]{3,2,1,0:T(8,128)(2,1)} %pad_maximum_fusion.17), channel_id=1, source_target_pairs={{0,4},{4,0},{8,12},{12,8},{1,5},{5,1},{9,13},{13,9},{2,6},{6,2},{1... | collective-permute-start | bytes 9437192 | tf_op jit(solution)/shard_map/ppermute | solution.py:271
  382.5 37.9 %collective-permute-start.35 = (bf16[2048,512]{1,0:T(8,128)(2,1)}, bf16[2048,512]{1,0:T(8,128)(2,1)}, u32[]{:S(2)}, u32[]{:S(2)}) collective-permute-start(bf16[2048,512]{1,0:T(8,128)(2,1)} %pad_maximum_fusion.25.refs_3_), channel_id=1, source_target_pairs={{0,4},{4,0},{8,12},{12,8},{1,5},{5,1},{9,13},{13,9},{2,6},{6,2},{1... | collective-permute-start | bytes 6291464 | tf_op jit(solution)/shard_map/ppermute | solution.py:271
  386.9 33.5 %collective-permute-start.32 = (bf16[1024,512]{1,0:T(8,128)(2,1)}, bf16[1024,512]{1,0:T(8,128)(2,1)}, u32[]{:S(2)}, u32[]{:S(2)}) collective-permute-start(bf16[1024,512]{1,0:T(8,128)(2,1)} %get-tuple-element.8149), channel_id=1, source_target_pairs={{0,8},{4,12},{9,1},{13,5},{18,26},{22,30},{27,19},{31,23},{8,24},{... | collective-permute-start | bytes 3145736 | tf_op jit(solution)/shard_map/ppermute | solution.py:471
  389.6 30.9 %collective-permute-start.31 = (bf16[1024,512]{1,0:T(8,128)(2,1)}, bf16[1024,512]{1,0:T(8,128)(2,1)}, u32[]{:S(2)}, u32[]{:S(2)}) collective-permute-start(bf16[1024,512]{1,0:T(8,128)(2,1)} %get-tuple-element.8150), channel_id=1, source_target_pairs={{0,16},{4,20},{9,25},{13,29},{18,2},{22,6},{27,11},{31,15},{16,24}... | collective-permute-start | bytes 3145736 | tf_op jit(solution)/shard_map/ppermute | solution.py:471
  424.3 28.3 %collective-permute-start.37 = (bf16[1024,512]{1,0:T(8,128)(2,1)}, bf16[1024,512]{1,0:T(8,128)(2,1)S(1)}, u32[]{:S(2)}, u32[]{:S(2)}) collective-permute-start(bf16[1024,512]{1,0:T(8,128)(2,1)} %get-tuple-element.8145), channel_id=1, source_target_pairs={{0,8},{4,12},{9,1},{13,5},{18,26},{22,30},{27,19},{31,23},{8,24},{... | collective-permute-start | bytes 3145736 | tf_op jit(solution)/shard_map/ppermute | solution.py:471
  429.8 26.9 %collective-permute-start.36 = (bf16[1024,512]{1,0:T(8,128)(2,1)}, bf16[1024,512]{1,0:T(8,128)(2,1)S(1)}, u32[]{:S(2)}, u32[]{:S(2)}) collective-permute-start(bf16[1024,512]{1,0:T(8,128)(2,1)} %get-tuple-element.8146), channel_id=1, source_target_pairs={{0,16},{4,20},{9,25},{13,29},{18,2},{22,6},{27,11},{31,15},{16,24}... | collective-permute-start | bytes 3145736 | tf_op jit(solution)/shard_map/ppermute | solution.py:471
  462.2 34.6 %collective-permute-start.40 = (bf16[2048,512]{1,0:T(8,128)(2,1)}, bf16[2048,512]{1,0:T(8,128)(2,1)}, u32[]{:S(2)}, u32[]{:S(2)}) collective-permute-start(bf16[2048,512]{1,0:T(8,128)(2,1)} %pad_maximum_fusion.26.refs_4_), channel_id=1, source_target_pairs={{0,4},{4,0},{8,12},{12,8},{1,5},{5,1},{9,13},{13,9},{2,6},{6,2},{1... | collective-permute-start | bytes 6291464 | tf_op jit(solution)/shard_map/ppermute | solution.py:271
  464.1 32.7 %collective-permute-start.41 = (bf16[2048,512]{1,0:T(8,128)(2,1)}, bf16[2048,512]{1,0:T(8,128)(2,1)}, u32[]{:S(2)}, u32[]{:S(2)}) collective-permute-start(bf16[2048,512]{1,0:T(8,128)(2,1)} %pad_maximum_fusion.27.refs_5_), channel_id=1, source_target_pairs={{0,4},{4,0},{8,12},{12,8},{1,5},{5,1},{9,13},{13,9},{2,6},{6,2},{1... | collective-permute-start | bytes 6291464 | tf_op jit(solution)/shard_map/ppermute | solution.py:271
  468.9 26.6 %collective-permute-start.38 = (bf16[1024,512]{1,0:T(8,128)(2,1)}, bf16[1024,512]{1,0:T(8,128)(2,1)S(1)}, u32[]{:S(2)}, u32[]{:S(2)}) collective-permute-start(bf16[1024,512]{1,0:T(8,128)(2,1)} %get-tuple-element.8138), channel_id=1, source_target_pairs={{0,16},{4,20},{9,25},{13,29},{18,2},{22,6},{27,11},{31,15},{16,24}... | collective-permute-start | bytes 3145736 | tf_op jit(solution)/shard_map/ppermute | solution.py:471
  470.2 26.6 %collective-permute-start.39 = (bf16[1024,512]{1,0:T(8,128)(2,1)}, bf16[1024,512]{1,0:T(8,128)(2,1)}, u32[]{:S(2)}, u32[]{:S(2)}) collective-permute-start(bf16[1024,512]{1,0:T(8,128)(2,1)} %get-tuple-element.8139), channel_id=1, source_target_pairs={{0,8},{4,12},{9,1},{13,5},{18,26},{22,30},{27,19},{31,23},{8,24},{... | collective-permute-start | bytes 3145736 | tf_op jit(solution)/shard_map/ppermute | solution.py:471
  474.2 68.2 %collective-permute-start.45 = (bf16[1024,512]{1,0:T(8,128)(2,1)}, bf16[1024,512]{1,0:T(8,128)(2,1)}, u32[]{:S(2)}, u32[]{:S(2)}) collective-permute-start(bf16[1024,512]{1,0:T(8,128)(2,1)} %get-tuple-element.8137), channel_id=1, source_target_pairs={{0,16},{4,20},{9,25},{13,29},{18,2},{22,6},{27,11},{31,15}} | collective-permute-start | bytes 3145736 | tf_op jit(solution)/shard_map/ppermute | solution.py:471
  495.5 46.9 %collective-permute-start.44 = (bf16[1024,512]{1,0:T(8,128)(2,1)}, bf16[1024,512]{1,0:T(8,128)(2,1)}, u32[]{:S(2)}, u32[]{:S(2)}) collective-permute-start(bf16[1024,512]{1,0:T(8,128)(2,1)} %get-tuple-element.8140), channel_id=1, source_target_pairs={{0,8},{4,12},{9,1},{13,5},{18,26},{22,30},{27,19},{31,23}} | collective-permute-start | bytes 3145736 | tf_op jit(solution)/shard_map/ppermute | solution.py:471
  496.8 45.6 %collective-permute-start.42 = (bf16[1024,512]{1,0:T(8,128)(2,1)S(1)}, bf16[1024,512]{1,0:T(8,128)(2,1)}, u32[]{:S(2)}, u32[]{:S(2)}) collective-permute-start(bf16[1024,512]{1,0:T(8,128)(2,1)S(1)} %collective-permute-done.38), channel_id=1, source_target_pairs={{16,24},{20,28},{25,17},{29,21},{2,10},{6,14},{11,3},{15,7},{24,8}... | collective-permute-start | bytes 3145736 | tf_op jit(solution)/shard_map/ppermute | solution.py:471
  498.1 44.3 %collective-permute-start.43 = (bf16[1024,512]{1,0:T(8,128)(2,1)}, bf16[1024,512]{1,0:T(8,128)(2,1)}, u32[]{:S(2)}, u32[]{:S(2)}) collective-permute-start(bf16[1024,512]{1,0:T(8,128)(2,1)} %collective-permute-done.39), channel_id=1, source_target_pairs={{8,24},{12,28},{1,17},{5,21},{26,10},{30,14},{19,3},{23,7},{24,16}... | collective-permute-start | bytes 3145736 | tf_op jit(solution)/shard_map/ppermute | solution.py:471
  (39 other events, 882.8 us)
Sparse Core Ops, SparseCore 0:
  13.3 47.1 all-gather.6
  182.4 46.4 all-gather.10
  230.5 44.6 all-gather.12
  276.6 44.6 all-gather.8
  322.7 44.6 all-gather.14
  391.0 47.0 all-gather.16
